TPU v7x, 128 devices: a whole 4x4x4 slice. The times are simulated.
128 devices in a mesh: node: 8 (over z, core), local: 16 (over y, x).
Axes of the slice: x: 4, y: 4, z: 4, core: 2. Of those that a mesh axis runs over, the one named last changes fastest.
Arguments:
- latent_cache: bfloat16 [64, 576, 2048], P('node', None, 'local'), may hold values from -6 to 6
- lengths: int32 [64], replicated, may hold values from 512 to 2048, as said below
- owner_map: int32 [64], replicated, may hold values from 0 to 127, as said below
- queries: bfloat16 [128, 2, 73728], P(('node', 'local')), may hold values from -15 to 15, as said below
- new_latent: bfloat16 [128, 2, 576], P(('node', 'local')), may hold values from -6 to 6, as said below
- residual: bfloat16 [128, 2, 7168], P(('node', 'local')), may hold values from -6 to 6
- w_value: bfloat16 [128, 512, 128], P(('node', 'local')), may hold values from -4 to 4
- w_out: bfloat16 [16384, 7168], P(('node', 'local')), may hold values from -0.046875 to 0.046875
- norm_gain: float32 [7168], replicated, may hold values from 0.1 to 1.9
- w_router: float32 [7168, 16], replicated, may hold values from -0.0625 to 0.0625
- expert_ids: int32 [128, 2, 8], P(('node', 'local')), may hold values from 0 to 15, all different within a row
- w_gate: bfloat16 [7168, 32768], P(None, ('node', 'local')), may hold values from -0.0625 to 0.0625
- w_up: bfloat16 [7168, 32768], P(None, ('node', 'local')), may hold values from -0.0625 to 0.0625
- w_down: bfloat16 [32768, 7168], P(('node', 'local')), may hold values from -0.125 to 0.125
Outputs:
- mixed: bfloat16 [128, 2, 7168], P(('node', 'local'))
Inputs may be any that keep to these rules, and one draw needn't show every extreme that they name: `lengths`: the longest request fills all 2048 positions; every request holds 512 or more. owner_map[r] is node index * 16 + local index of the device that serves request r; requests 8 * n to 8 * n + 7 are those prefilled on node n. No device serves two requests. The requests prefilled on one node are served by devices of distinct local indices, exactly 1 of them on each node, and the same 8 local indices serve on every node; local indices 0 and 15 are among them. `queries`: rows of devices that serve no request are not read. `new_latent`: rows of devices that serve no request are not read.
All inputs are finite; a program needn't handle non-finite values.
Results may differ from a plain program's by a relative error of at most 0.0095.
Values may be sent and summed in bfloat16 or wider, within the bound.
A program may use at most 128 MiB of HBM per device.

v0:
```python
import jax
import jax.numpy as jnp
from jax import lax
from jax.sharding import PartitionSpec as P

LAT = 512


score_scale = 192.0 ** (-0.5)
route_scale = 2.5
norm_eps = 1e-06


def attend_request(key_rows, query_rows, fresh_rows, length):
    step_count = fresh_rows.shape[0]
    key_width = fresh_rows.shape[1]
    head_count = query_rows.shape[1] // key_width
    flat_rows = query_rows.reshape(step_count * head_count, key_width)
    cached = jnp.dot(flat_rows, key_rows, preferred_element_type=jnp.float32) * score_scale
    places = jnp.arange(key_rows.shape[1], dtype=jnp.int32)
    cached = jnp.where(places[None, :] < length, cached, -jnp.inf)
    fresh_scores = (
        lax.dot_general(
            flat_rows, fresh_rows, (((1,), (1,)), ((), ())), preferred_element_type=jnp.float32
        )
        * score_scale
    )
    row_step = jnp.arange(step_count * head_count, dtype=jnp.int32) // head_count
    col_step = jnp.arange(step_count, dtype=jnp.int32)
    fresh_scores = jnp.where(col_step[None, :] <= row_step[:, None], fresh_scores, -jnp.inf)
    row_max = jnp.maximum(jnp.max(cached, axis=1), jnp.max(fresh_scores, axis=1))
    cache_weights = jnp.exp(cached - row_max[:, None])
    fresh_weights = jnp.exp(fresh_scores - row_max[:, None])
    weight_total = jnp.sum(cache_weights, axis=1) + jnp.sum(fresh_weights, axis=1)
    weighted = lax.dot_general(
        cache_weights.astype(jnp.bfloat16),
        key_rows[:LAT],
        (((1,), (1,)), ((), ())),
        preferred_element_type=jnp.float32,
    )
    weighted = weighted + jnp.dot(
        fresh_weights.astype(jnp.bfloat16), fresh_rows[:, :LAT], preferred_element_type=jnp.float32
    )
    result = (weighted / weight_total[:, None]).astype(jnp.bfloat16)
    return jnp.transpose(result.reshape(step_count, head_count, LAT), (1, 0, 2))


def expert_rows(token_rows, gate_part, up_part, down_part):
    gated = jnp.dot(token_rows, gate_part, preferred_element_type=jnp.float32)
    lifted = jnp.dot(token_rows, up_part, preferred_element_type=jnp.float32)
    middle = (jax.nn.silu(gated) * lifted).astype(jnp.bfloat16)
    return jnp.dot(middle, down_part, preferred_element_type=jnp.float32)


def shards(
    latent_cache,
    lengths,
    owner_map,
    queries,
    new_latent,
    residual,
    w_value,
    w_out,
    norm_gain,
    w_router,
    expert_ids,
    w_gate,
    w_up,
    w_down,
):
    node_count = lax.axis_size("node")
    local_count = lax.axis_size("local")
    device_count = node_count * local_count
    node_here = lax.axis_index("node")
    local_here = lax.axis_index("local")
    device_here = node_here * local_count + local_here
    total_requests = owner_map.shape[0]
    node_requests = total_requests // node_count
    pair_count = node_requests // node_count
    key_width = latent_cache.shape[1]
    span_len = latent_cache.shape[2]
    request_ids = jnp.arange(total_requests, dtype=jnp.int32)
    target_node = owner_map // local_count
    source_node = request_ids // node_requests
    same_route = (source_node[None, :] == source_node[:, None]) & (
        target_node[None, :] == target_node[:, None]
    )
    earlier = same_route & (request_ids[None, :] < request_ids[:, None])
    route_rank = jnp.sum(earlier.astype(jnp.int32), axis=1)
    node_start = node_here * node_requests
    local_target = lax.dynamic_slice_in_dim(target_node, node_start, node_requests)
    local_rank = lax.dynamic_slice_in_dim(route_rank, node_start, node_requests)
    slot_of = local_target * pair_count + local_rank
    picked = (
        jnp.zeros((node_requests,), jnp.int32)
        .at[slot_of]
        .set(jnp.arange(node_requests, dtype=jnp.int32))
    )
    outgoing = jnp.take(latent_cache, picked, axis=0).reshape(
        node_count, pair_count, key_width, span_len
    )
    arrived = lax.all_to_all(outgoing, "node", split_axis=0, concat_axis=0, tiled=True)
    item_key = jnp.where(
        target_node == node_here, source_node * pair_count + route_rank, node_count * pair_count
    )
    item_request = (
        jnp.zeros((node_count * pair_count,), jnp.int32).at[item_key].set(request_ids, mode="drop")
    )
    item_local = jnp.take(owner_map, item_request) % local_count
    sectioned = (
        jnp.zeros((local_count, key_width, span_len), jnp.bfloat16)
        .at[item_local]
        .set(arrived.reshape(node_count * pair_count, key_width, span_len))
    )
    gathered_keys = lax.all_to_all(sectioned, "local", split_axis=0, concat_axis=2, tiled=True)
    owned_mask = owner_map == device_here
    has_request = jnp.any(owned_mask)
    request_here = jnp.argmax(owned_mask)
    length = jnp.where(has_request, jnp.take(lengths, request_here), 0)
    attended = attend_request(gathered_keys[0], queries[0], new_latent[0], length)
    attended = jnp.where(has_request, attended, jnp.zeros_like(attended))
    step_count = attended.shape[1]
    heads_here = attended.shape[0] // device_count
    by_head = attended.reshape(device_count, heads_here, step_count, attended.shape[2])
    received = lax.all_to_all(by_head, ("node", "local"), split_axis=0, concat_axis=0, tiled=True)
    head_values = jnp.einsum(
        "shtl,hlv->shtv", received, w_value, preferred_element_type=jnp.float32
    ).astype(jnp.bfloat16)
    value_rows = jnp.transpose(head_values, (0, 2, 1, 3)).reshape(
        device_count * step_count, heads_here * head_values.shape[3]
    )
    attention = lax.psum_scatter(
        jnp.dot(value_rows, w_out, preferred_element_type=jnp.float32),
        ("node", "local"),
        scatter_dimension=0,
        tiled=True,
    )
    hidden = (residual[0].astype(jnp.float32) + attention).astype(jnp.bfloat16)
    hidden_wide = hidden.astype(jnp.float32)
    normed = (
        hidden_wide
        * lax.rsqrt(jnp.mean(hidden_wide * hidden_wide, axis=-1, keepdims=True) + norm_eps)
        * norm_gain
    ).astype(jnp.bfloat16)
    expert_count = w_router.shape[1]
    per_node = expert_count // node_count
    group_size = local_count // per_node
    slot_here = local_here // group_size
    affinity = jax.nn.sigmoid(
        jnp.dot(normed.astype(jnp.float32), w_router, precision=lax.Precision.HIGHEST)
    )
    choose = (expert_ids[0][:, :, None] == jnp.arange(expert_count, dtype=jnp.int32)).astype(
        jnp.float32
    )
    picked_scores = jnp.sum(affinity[:, None, :] * choose, axis=2)
    gate_weights = picked_scores / jnp.sum(picked_scores, axis=1, keepdims=True) * route_scale
    combine = jnp.sum(gate_weights[:, :, None] * choose, axis=1).astype(jnp.bfloat16)
    node_weights = jnp.transpose(combine.reshape(step_count, node_count, per_node), (1, 0, 2))
    node_hits = (
        jnp.sum(jnp.sum(choose, axis=1).reshape(step_count, node_count, per_node), axis=2) > 0.0
    )
    outbound = jnp.where(
        jnp.transpose(node_hits)[:, :, None], normed[None, :, :], jnp.zeros((), jnp.bfloat16)
    )
    model_width = outbound.shape[2]
    spread = jnp.broadcast_to(
        outbound[:, None], (node_count, local_count, step_count, model_width)
    ).reshape(device_count, step_count, model_width)
    spread_weights = jnp.broadcast_to(
        node_weights[:, None], (node_count, local_count, step_count, per_node)
    ).reshape(device_count, step_count, per_node)
    landed, landed_weights = (
        lax.all_to_all(spread, ("node", "local"), split_axis=0, concat_axis=0, tiled=True),
        lax.all_to_all(spread_weights, ("node", "local"), split_axis=0, concat_axis=0, tiled=True),
    )
    part_out = expert_rows(landed.reshape(-1, model_width), w_gate, w_up, w_down).reshape(
        device_count, step_count, model_width
    )
    partial_value = part_out * lax.dynamic_slice_in_dim(landed_weights, slot_here, 1, 2).astype(
        jnp.float32
    )
    returned = lax.all_to_all(
        partial_value.astype(jnp.bfloat16),
        ("node", "local"),
        split_axis=0,
        concat_axis=0,
        tiled=True,
    ).astype(partial_value.dtype)
    results = jnp.sum(
        returned.reshape(node_count, local_count, step_count, model_width), axis=1
    ).astype(jnp.bfloat16)
    mixture = jnp.sum(results.astype(jnp.float32), axis=0)
    mixed = (hidden_wide + mixture).astype(jnp.bfloat16)
    return mixed[None]


def solution(mesh):
    in_specs = (
        P("node", None, "local"),
        P(),
        P(),
        P(("node", "local"), None, None),
        P(("node", "local"), None, None),
        P(("node", "local"), None, None),
        P(("node", "local"), None, None),
        P(("node", "local"), None),
        P(),
        P(),
        P(("node", "local"), None, None),
        P(None, ("node", "local")),
        P(None, ("node", "local")),
        P(("node", "local"), None),
    )
    out_specs = P(("node", "local"), None, None)
    return jax.shard_map(shards, mesh=mesh, in_specs=in_specs, out_specs=out_specs, check_vma=False)
```

profile of v0, /device:TPU:1, one launch (start us, length us, event | category | flops | bytes accessed | tf_op | source)
XLA Modules:
  0.0 453.8 jit_solution(8875903236552119249)
XLA Ops:
  11.5 6.8 %all-to-all-start = ((bf16[8,1,576,128]{3,2,1,0:T(8,128)(2,1)}), bf16[8,1,576,128]{3,2,1,0:T(8,128)(2,1)S(1)}, u32[]{:S(2)}, u32[]{:S(2)}) async-start(bf16[8,1,576,128]{3,2,1,0:T(8,128)(2,1)} %fusion.7), calls=%async_computation | async-start | bytes 2359296 | tf_op jit(solution)/shard_map/all_to_all | solution.py:102
  19.8 15.0 %all-to-all-done = bf16[8,1,576,128]{3,2,1,0:T(8,128)(2,1)S(1)} async-done(((bf16[8,1,576,128]{3,2,1,0:T(8,128)(2,1)}), bf16[8,1,576,128]{3,2,1,0:T(8,128)(2,1)S(1)}, u32[]{:S(2)}, u32[]{:S(2)}) %all-to-all-start) | async-done | bytes 1179680 | tf_op jit(solution)/shard_map/all_to_all | solution.py:102
  36.7 3.1 scatter_fusion
  39.7 6.9 %all-to-all-start.1 = ((bf16[16,576,128]{2,1,0:T(8,128)(2,1)}), bf16[16,576,128]{2,1,0:T(8,128)(2,1)}, u32[]{:S(2)}, u32[]{:S(2)}) async-start(bf16[16,576,128]{2,1,0:T(8,128)(2,1)} %scatter_fusion), calls=%async_computation.1 | async-start | bytes 4718592 | tf_op jit(solution)/shard_map/all_to_all | solution.py:115
  52.0 28.6 %all-to-all-done.1 = bf16[16,576,128]{2,1,0:T(8,128)(2,1)} async-done(((bf16[16,576,128]{2,1,0:T(8,128)(2,1)}), bf16[16,576,128]{2,1,0:T(8,128)(2,1)}, u32[]{:S(2)}, u32[]{:S(2)}) %all-to-all-start.1) | async-done | bytes 2359328 | tf_op jit(solution)/shard_map/all_to_all | solution.py:115
  80.6 3.2 copy.52
  83.8 3.1 slice.21
  90.3 3.9 copy.53
  94.2 3.7 fusion.8
  98.2 17.2 %all_to_all.40 = bf16[128,1,2,512]{3,2,1,0:T(2,128)(2,1)S(1)} all-to-all(bf16[128,1,2,512]{3,2,1,0:T(2,128)(2,1)S(1)} %bitcast.76), channel_id=1, replica_groups=mesh['node'=8,'local'=16] {'node','local'}, dimensions={0} | all-to-all | bytes 524288 | tf_op jit(solution)/shard_map/all_to_all | solution.py:125
  115.7 4.1 fusion.50
  119.9 155.9 %all-reduce.3.cloned.1.call-done = f32[256,7168]{1,0:T(8,128)} async-done(((f32[256,7168]{1,0:T(8,128)}), f32[256,7168]{1,0:T(8,128)}) %all-reduce.3.cloned.1.call-update) | async-done | bytes 7340048
  279.1 6.7 %all-to-all-start.4 = ((bf16[128,2,2]{1,2,0:T(2,128)(2,1)}), bf16[128,2,2]{1,2,0:T(2,128)(2,1)S(1)}, u32[]{:S(2)}, u32[]{:S(2)}) async-start(bf16[128,2,2]{1,2,0:T(2,128)(2,1)} %bitcast.25), calls=%async_computation.4 | async-start | bytes 131072 | tf_op jit(solution)/shard_map/all_to_all | solution.py:174
  286.0 9.4 %all-to-all-done.4 = bf16[128,2,2]{1,2,0:T(2,128)(2,1)S(1)} async-done(((bf16[128,2,2]{1,2,0:T(2,128)(2,1)}), bf16[128,2,2]{1,2,0:T(2,128)(2,1)S(1)}, u32[]{:S(2)}, u32[]{:S(2)}) %all-to-all-start.4) | async-done | bytes 1056 | tf_op jit(solution)/shard_map/all_to_all | solution.py:174
  295.3 3.7 broadcast_in_dim.121
  299.0 5.4 %all-to-all-start.3 = ((bf16[128,2,7168]{2,1,0:T(2,128)(2,1)}), bf16[128,2,7168]{2,1,0:T(2,128)(2,1)}, u32[]{:S(2)}, u32[]{:S(2)}) async-start(bf16[128,2,7168]{2,1,0:T(2,128)(2,1)} %bitcast.72), calls=%async_computation.3 | async-start | bytes 7340032 | tf_op jit(solution)/shard_map/all_to_all | solution.py:173
  304.6 46.0 %all-to-all-done.3 = bf16[128,2,7168]{2,1,0:T(2,128)(2,1)} async-done(((bf16[128,2,7168]{2,1,0:T(2,128)(2,1)}), bf16[128,2,7168]{2,1,0:T(2,128)(2,1)}, u32[]{:S(2)}, u32[]{:S(2)}) %all-to-all-start.3) | async-done | bytes 3670048 | tf_op jit(solution)/shard_map/all_to_all | solution.py:173
  350.6 8.4 %reshape.177 = bf16[256,7168]{1,0:T(8,128)(2,1)} reshape(bf16[128,2,7168]{2,1,0:T(2,128)(2,1)} %all-to-all-done.3) | data formatting | bytes 7340032 | tf_op jit(solution)/shard_map/reshape | solution.py:176
  359.0 4.3 fusion.51
  363.3 11.2 %fusion.10 = f32[256,7168]{1,0:T(8,128)} fusion(bf16[256,7168]{1,0:T(8,128)(2,1)} %param.27, bf16[256,7168]{1,0:T(8,128)(2,1)} %reshape.177, bf16[7168,256]{1,0:T(8,128)(2,1)} %param.26, f32[256,256]{1,0:T(8,128)S(1)} %fusion.51), kind=kOutput, calls=%fused_computation.22 | convolution fusion | flops 1879441408 | bytes 18612224 | tf_op jit(solution)/shard_map/dot_general | solution.py:52
  374.4 9.3 %reshape.178 = f32[128,2,7168]{2,1,0:T(2,128)} reshape(f32[256,7168]{1,0:T(8,128)} %fusion.10) | data formatting | bytes 14680064 | tf_op jit(solution)/shard_map/reshape | solution.py:176
  383.7 8.0 %multiply_convert_fusion = bf16[128,2,7168]{2,1,0:T(2,128)(2,1)} fusion(f32[128,2,7168]{2,1,0:T(2,128)} %reshape.178, f32[128,2]{1,0:T(8,128)S(1)} %bitcast.77), kind=kLoop, calls=%fused_computation.5 | loop fusion | flops 3670016 | bytes 11011072 | tf_op jit(solution)/shard_map/convert_element_type | solution.py:183
  391.7 51.3 %all_to_all.41 = bf16[128,2,7168]{2,1,0:T(2,128)(2,1)S(1)} all-to-all(bf16[128,2,7168]{2,1,0:T(2,128)(2,1)} %multiply_convert_fusion), channel_id=1, replica_groups=mesh['node'=8,'local'=16] {'node','local'}, dimensions={0} | all-to-all | bytes 7340032 | tf_op jit(solution)/shard_map/all_to_all | solution.py:182
  443.0 3.1 bitcast_reduce_fusion
  (78 shorter events, 18.9 us)
Async XLA Ops:
  6.5 109.2 %copy-start = (bf16[128,7168]{1,0:T(8,128)(2,1)S(1)}, bf16[128,7168]{1,0:T(8,128)(2,1)}, u32[]{:S(2)}) copy-start(bf16[128,7168]{1,0:T(8,128)(2,1)} %param.21) | copy-start | bytes 5505028
  10.3 8.8 %copy-start.2 = (s32[64]{0:T(128)S(1)}, s32[64]{0:T(128)}, u32[]{:S(2)}) copy-start(s32[64]{0:T(128)} %param.16) | copy-start | bytes 772
  11.5 23.3 %all-to-all-start = ((bf16[8,1,576,128]{3,2,1,0:T(8,128)(2,1)}), bf16[8,1,576,128]{3,2,1,0:T(8,128)(2,1)S(1)}, u32[]{:S(2)}, u32[]{:S(2)}) async-start(bf16[8,1,576,128]{3,2,1,0:T(8,128)(2,1)} %fusion.7), calls=%async_computation | async-start | bytes 2359296 | tf_op jit(solution)/shard_map/all_to_all | solution.py:102
  39.7 9.3 %copy-start.11 = (s32[64]{0:T(128)S(1)}, s32[64]{0:T(128)}, u32[]{:S(2)}) copy-start(s32[64]{0:T(128)} %param.15) | copy-start | bytes 772
  39.7 9.9 %copy-start.5 = (bf16[1,2,73728]{2,1,0:T(2,128)(2,1)S(1)}, bf16[1,2,73728]{2,1,0:T(2,128)(2,1)}, u32[]{:S(2)}) copy-start(bf16[1,2,73728]{2,1,0:T(2,128)(2,1)} %param.17) | copy-start | bytes 884740
  39.7 12.1 %copy-start.8 = (bf16[1,2,576]{2,1,0:T(2,128)(2,1)S(1)}, bf16[1,2,576]{2,1,0:T(2,128)(2,1)}, u32[]{:S(2)}) copy-start(bf16[1,2,576]{2,1,0:T(2,128)(2,1)} %param.18) | copy-start | bytes 6916
  39.7 40.9 %all-to-all-start.1 = ((bf16[16,576,128]{2,1,0:T(8,128)(2,1)}), bf16[16,576,128]{2,1,0:T(8,128)(2,1)}, u32[]{:S(2)}, u32[]{:S(2)}) async-start(bf16[16,576,128]{2,1,0:T(8,128)(2,1)} %scatter_fusion), calls=%async_computation.1 | async-start | bytes 4718592 | tf_op jit(solution)/shard_map/all_to_all | solution.py:115
  46.7 229.2 %all-reduce.3.cloned.1.call-start = ((), (), s32[]{:S(2)}) async-start(), calls=%async_computation.6 | async-start | bytes 14680064
  88.3 1.3 copy-start.3
  94.2 21.2 %copy-start.10 = (bf16[1,512,128]{2,1,0:T(8,128)(2,1)S(1)}, bf16[1,512,128]{2,1,0:T(8,128)(2,1)}, u32[]{:S(2)}) copy-start(bf16[1,512,128]{2,1,0:T(8,128)(2,1)} %param.20) | copy-start | bytes 393220
  119.9 156.0 %copy-start.6 = (bf16[1,2,7168]{2,1,0:T(2,128)(2,1)S(1)}, bf16[1,2,7168]{2,1,0:T(2,128)(2,1)}, u32[]{:S(2)}) copy-start(bf16[1,2,7168]{2,1,0:T(2,128)(2,1)} %param.19) | copy-start | bytes 86020
  119.9 157.1 %copy-start.7 = (f32[7168]{0:T(1024)S(1)}, f32[7168]{0:T(1024)}, u32[]{:S(2)}) copy-start(f32[7168]{0:T(1024)} %param.22) | copy-start | bytes 86020
  119.9 157.2 %copy-start.4 = (f32[7168,16]{0,1:T(8,128)S(1)}, f32[7168,16]{0,1:T(8,128)}, u32[]{:S(2)}) copy-start(f32[7168,16]{0,1:T(8,128)} %param.23) | copy-start | bytes 1376260
  119.9 157.6 %copy-start.9 = (s32[1,2,8]{2,1,0:T(2,128)S(1)}, s32[1,2,8]{2,1,0:T(2,128)}, u32[]{:S(2)}) copy-start(s32[1,2,8]{2,1,0:T(2,128)} %param.24) | copy-start | bytes 196
  279.1 16.3 %all-to-all-start.4 = ((bf16[128,2,2]{1,2,0:T(2,128)(2,1)}), bf16[128,2,2]{1,2,0:T(2,128)(2,1)S(1)}, u32[]{:S(2)}, u32[]{:S(2)}) async-start(bf16[128,2,2]{1,2,0:T(2,128)(2,1)} %bitcast.25), calls=%async_computation.4 | async-start | bytes 131072 | tf_op jit(solution)/shard_map/all_to_all | solution.py:174
  299.0 51.6 %all-to-all-start.3 = ((bf16[128,2,7168]{2,1,0:T(2,128)(2,1)}), bf16[128,2,7168]{2,1,0:T(2,128)(2,1)}, u32[]{:S(2)}, u32[]{:S(2)}) async-start(bf16[128,2,7168]{2,1,0:T(2,128)(2,1)} %bitcast.72), calls=%async_computation.3 | async-start | bytes 7340032 | tf_op jit(solution)/shard_map/all_to_all | solution.py:173
  391.7 55.3 %copy-start.1 = (bf16[128,7168]{1,0:T(8,128)(2,1)S(1)}, bf16[128,7168]{1,0:T(8,128)(2,1)}, u32[]{:S(2)}) copy-start(bf16[128,7168]{1,0:T(8,128)(2,1)} %param.21) | copy-start | bytes 5505028
Sparse Core Ops, SparseCore 0:
  120.0 155.7 all-reduce.2
where the time goes:
time: 455 us; the launch traced here: 454 us
  waiting for transfers between devices  255 us (56%)
  blocking collectives  68.6 us (15%)
  local copies, waits for them, and re-layouts  44.3 us (10%)
  starting transfers between devices  25.9 us (6%)
  matrix products  25.7 us (6%)
  other arithmetic  17.8 us (4%)
  between operations  16.6 us (4%)
    unnamed x2, waiting for transfers between devices  156 us
    all_to_all x1, blocking collectives, shards(): lax.all_to_all(partial_value.astype(jnp.bfloat16), ('node', 'local'), spl...  51.3 us
    all_to_all x1, waiting for transfers between devices, shards(): lax.all_to_all(spread, ('node', 'local'), split_axis=0, concat_axis=0, ti...  46 us
    all_to_all x1, waiting for transfers between devices, shards(): lax.all_to_all(sectioned, 'local', split_axis=0, concat_axis=2, tiled=True)  28.6 us
    all_to_all x1, blocking collectives, shards(): lax.all_to_all(by_head, ('node', 'local'), split_axis=0, concat_axis=0, t...  17.2 us
    all_to_all x1, waiting for transfers between devices, shards(): lax.all_to_all(outgoing, 'node', split_axis=0, concat_axis=0, tiled=True)  15 us
    dot_general x1, matrix products, expert_rows(): return jnp.dot(middle, down_part, preferred_element_type=jnp.float32)  11.2 us
    all_to_all x1, waiting for transfers between devices, shards(): lax.all_to_all(spread_weights, ('node', 'local'), split_axis=0, concat_ax...  9.35 us
  transfers between devices with their start and end apart: 5, of which 5 were waited for; matrix products, arithmetic and copies ran while one was open for 1% of the time, Pallas kernels for 0%

commit v1 on v0

v1 whole, which is shorter than its diff:
```python
import functools

import jax
import jax.numpy as jnp
from jax import lax
from jax.experimental import pallas as pl
from jax.experimental.pallas import tpu as pltpu
from jax.sharding import PartitionSpec as P

MESH = pl.DeviceIdType.MESH
BF = jnp.bfloat16
F32 = jnp.float32
score_scale = 192.0 ** (-0.5)
route_scale = 2.5
norm_eps = 1e-06
NT = (((1,), (1,)), ((), ()))


def iota(shape, dim):
    return lax.broadcasted_iota(jnp.int32, shape, dim)


def landed(ref, sem):
    pltpu.make_async_copy(ref, ref, sem).wait()


def send(src, dst, send_sem, recv_sem, device):
    pltpu.make_async_remote_copy(
        src_ref=src, dst_ref=dst, send_sem=send_sem, recv_sem=recv_sem,
        device_id=device, device_id_type=MESH,
    ).start()


def keep(src, dst, sem):
    pltpu.make_async_copy(src, dst, sem).start()


def home_local(node, target):
    row = target // 2
    return row * 4 + (target % 2) * 2 + (row + node) % 2


def each(lo, hi, body):
    def step(i, carry):
        body(i)
        return carry
    lax.fori_loop(lo, hi, step, 0)


def attend_kernel(
    owner, lengths, cache, qc, w_value, w_out, out,
    csend, crecv, q1, q2s, q2, q3, sbuf, acc, att, c1, c2s, c2, hv, hvr, wr, ys, yr,
    cs, cr, q1s, q1r, q2ss, q2r, q3s, q3r, a1s, a1r, a2s, a2r, hs, hr, ws, wrr, yss, yrr,
):
    n = lax.axis_index("node")
    l = lax.axis_index("local")
    yy, xx, core, zz = l // 4, l % 4, n % 2, n // 2
    home_core = (xx + yy) % 2
    is_home = home_core == core

    bar = pltpu.get_barrier_semaphore()
    each(1, 16, lambda j: pl.semaphore_signal(bar, 1, device_id=(n, (l + j) % 16), device_id_type=MESH))
    each(1, 8, lambda j: pl.semaphore_signal(bar, 1, device_id=((n + j) % 8, l), device_id_type=MESH))
    pl.semaphore_wait(bar, 22)

    keep(qc.at[l], q1.at[l], q1r.at[l])

    def q_first(j):
        p = (l + j) % 16
        send(qc.at[p], q1.at[l], q1s.at[p], q1r.at[l], (n, p))
    each(1, 16, q_first)

    def cache_send(j):
        t = (l + j) % 8
        pick = jnp.int32(0)
        for i in range(8):
            pick = jnp.where(owner[n * 8 + i] // 16 == t, i, pick)
        csend[t] = cache[pick]
        dest = home_local(n, t)

        @pl.when(dest == l)
        def _():
            keep(csend.at[t], crecv.at[l], cr.at[l])

        @pl.when(dest != l)
        def _():
            send(csend.at[t], crecv.at[l], cs.at[t], cr.at[l], (n, dest))
    each(0, 8, cache_send)

    def w_send(j):
        p = (n + j) % 8
        send(w_out.at[:, pl.ds(pl.multiple_of(p * 896, 128), 896)], wr.at[n], ws.at[p], wrr.at[n], (p, l))
    keep(w_out.at[:, pl.ds(pl.multiple_of(n * 896, 128), 896)], wr.at[n], wrr.at[n])
    each(1, 8, w_send)

    each(0, 16, lambda j: landed(q1.at[j], q1r.at[j]))

    def q_second(j):
        p = (n + j) % 8
        pick = jnp.int32(0)
        for i in range(8):
            o = owner[p * 8 + i]
            pick = jnp.where(o // 16 == n, o % 16, pick)
        q2s[p] = q1[pick]

        @pl.when(p == n)
        def _():
            keep(q2s.at[p], q2.at[n], q2r.at[n])

        @pl.when(p != n)
        def _():
            send(q2s.at[p], q2.at[n], q2ss.at[p], q2r.at[n], (p, l))
    each(0, 8, q_second)

    def q_third(j):
        t = (n + j) % 8
        landed(q2.at[t], q2r.at[t])
        dest = home_local(n, t)

        @pl.when(dest == l)
        def _():
            keep(q2.at[t], q3.at[l], q3r.at[l])

        @pl.when(dest != l)
        def _():
            send(q2.at[t], q3.at[l], q3s.at[t], q3r.at[l], (n, dest))
    each(0, 8, q_third)

    @pl.when(is_home)
    def _():
        each(0, 16, lambda j: landed(q3.at[j], q3r.at[j]))
        mine = yy * 2 + xx // 2
        length = jnp.int32(0)
        for i in range(8):
            r = n * 8 + i
            length = jnp.where(owner[r] // 16 == mine, lengths[r], length)
        q = q3[...].reshape(256, 640)[:, :576]
        spread = (iota((64, 576), 1) % 64 == iota((64, 576), 0)).astype(BF)
        own_band = iota((16, 576), 1) // 64 == iota((16, 576), 0)
        fresh = []
        for t in range(2):
            wide = jnp.dot(q3[t][:, 576:640], spread, preferred_element_type=F32)
            fresh.append(jnp.sum(jnp.where(own_band, wide, 0.0), axis=0, keepdims=True))
        line = iota((128, 576), 0)
        fresh_rows = jnp.where(line == 0, fresh[0], jnp.where(line == 1, fresh[1], 0.0)).astype(BF)
        fs = lax.dot_general(q, fresh_rows, NT, preferred_element_type=F32) * score_scale
        fs = jnp.where(iota((256, 128), 1) <= iota((256, 128), 0) % 2, fs, -jnp.inf)

        def score(p, top):
            landed(crecv.at[2 * p], cr.at[2 * p])
            landed(crecv.at[2 * p + 1], cr.at[2 * p + 1])
            keys = jnp.concatenate([crecv[2 * p], crecv[2 * p + 1]], axis=1)
            s = jnp.dot(q, keys, preferred_element_type=F32) * score_scale
            s = jnp.where(p * 256 + iota((256, 256), 1) < length, s, -jnp.inf)
            sbuf[p] = s
            return jnp.maximum(top, jnp.max(s, axis=1, keepdims=True))
        top = lax.fori_loop(0, 8, score, jnp.max(fs, axis=1, keepdims=True))
        fe = jnp.exp(fs - top)
        acc[...] = jnp.dot(fe.astype(BF), fresh_rows[:, :512], preferred_element_type=F32)

        def weigh(p, total):
            e = jnp.exp(sbuf[p] - top)
            values = jnp.concatenate([crecv[2 * p, :512, :], crecv[2 * p + 1, :512, :]], axis=1)
            acc[...] += lax.dot_general(e.astype(BF), values, NT, preferred_element_type=F32)
            return total + jnp.sum(e, axis=1, keepdims=True)
        total = lax.fori_loop(0, 8, weigh, jnp.sum(fe, axis=1, keepdims=True))
        att[...] = (acc[...] / total).astype(BF).reshape(8, 32, 512)

        keep(att.at[n], c1.at[zz], a1r.at[zz])

        def head_node(j):
            p = (n + j) % 8
            send(att.at[p], c1.at[zz], a1s.at[p], a1r.at[zz], (p, l))
        each(1, 8, head_node)

    each(0, 4, lambda j: landed(c1.at[j], a1r.at[j]))
    to = iota((128, 128), 0)
    perm = (iota((128, 128), 1) == (to // 2 % 4) * 32 + (to // 8) * 2 + to % 2).astype(BF)
    c2s[...] = jnp.dot(perm, c1[...].reshape(128, 512), preferred_element_type=F32).reshape(16, 8, 512)
    keep(c2s.at[l], c2.at[l], a2r.at[l])

    def head_local(j):
        p = (l + j) % 16
        send(c2s.at[p], c2.at[l], a2s.at[p], a2r.at[l], (n, p))
    each(1, 16, head_local)
    each(0, 16, lambda j: landed(c2.at[j], a2r.at[j]))
    hv[...] = jnp.dot(
        c2[...].reshape(128, 512).astype(BF), w_value[...], preferred_element_type=F32
    ).astype(BF)
    keep(hv, hvr.at[n], hr.at[n])

    def values_out(j):
        p = (n + j) % 8
        send(hv, hvr.at[n], hs.at[p], hr.at[n], (p, l))
    each(1, 8, values_out)
    each(0, 8, lambda j: landed(wr.at[j], wrr.at[j]))
    each(0, 8, lambda j: landed(hvr.at[j], hr.at[j]))
    lhs = jnp.concatenate([hvr[j] for j in range(8)], axis=1)
    ys[...] = jnp.dot(lhs, wr[...].reshape(1024, 896), preferred_element_type=F32).reshape(16, 8, 896)
    keep(ys.at[l], yr.at[l], yrr.at[l])

    def rows_out(j):
        p = (l + j) % 16
        send(ys.at[p], yr.at[l], yss.at[p], yrr.at[l], (n, p))
    each(1, 16, rows_out)
    each(0, 16, lambda j: landed(yr.at[j], yrr.at[j]))
    tot = yr[0]
    for j in range(1, 16):
        tot = tot + yr[j]
    low = tot[:, :512]
    high = jnp.concatenate([tot[:, 512:], jnp.zeros((8, 128), F32)], axis=1)
    out[...] = jnp.concatenate([low, high], axis=0).astype(BF)

    def drain(j):
        p = (l + j) % 16
        landed(qc.at[p], q1s.at[p])
        landed(c2s.at[p], a2s.at[p])
        landed(ys.at[p], yss.at[p])
    each(1, 16, drain)

    def drain_home(t):
        @pl.when(home_local(n, t) != l)
        def _():
            landed(csend.at[t], cs.at[t])
            landed(q2.at[t], q3s.at[t])
    each(0, 8, drain_home)

    def drain_node(j):
        p = (n + j) % 8
        landed(q2s.at[p], q2ss.at[p])
        landed(hv, hs.at[p])
        landed(wr.at[p], ws.at[p])

        @pl.when(is_home)
        def _():
            landed(att.at[p], a1s.at[p])
    each(1, 8, drain_node)


def attend(owner, lengths, cache, qc, w_value, w_out):
    dma = pltpu.SemaphoreType.DMA
    vm = pl.BlockSpec(memory_space=pltpu.VMEM)
    sm = pl.BlockSpec(memory_space=pltpu.SMEM)
    return pl.pallas_call(
        attend_kernel,
        name="attend",
        out_shape=jax.ShapeDtypeStruct((16, 512), BF),
        in_specs=[sm, sm, vm, vm, vm, pl.BlockSpec(memory_space=pl.ANY)],
        out_specs=vm,
        scratch_shapes=[
            pltpu.VMEM((8, 576, 128), BF),
            pltpu.VMEM((16, 576, 128), BF),
            pltpu.VMEM((16, 16, 640), BF),
            pltpu.VMEM((8, 16, 640), BF),
            pltpu.VMEM((8, 16, 640), BF),
            pltpu.VMEM((16, 16, 640), BF),
            pltpu.VMEM((8, 256, 256), F32),
            pltpu.VMEM((256, 512), F32),
            pltpu.VMEM((8, 32, 512), BF),
            pltpu.VMEM((4, 32, 512), BF),
            pltpu.VMEM((16, 8, 512), F32),
            pltpu.VMEM((16, 8, 512), F32),
            pltpu.VMEM((128, 128), BF),
            pltpu.VMEM((8, 128, 128), BF),
            pltpu.VMEM((8, 128, 896), BF),
            pltpu.VMEM((16, 8, 896), F32),
            pltpu.VMEM((16, 8, 896), F32),
        ] + [dma((k,)) for k in (8, 16, 16, 16, 8, 8, 8, 16, 8, 4, 16, 16, 8, 8, 8, 8, 16, 16)],
        compiler_params=pltpu.CompilerParams(
            collective_id=0, has_side_effects=True, vmem_limit_bytes=40 << 20
        ),
    )(owner, lengths, cache, qc, w_value, w_out)


GATHER = (("y", "z", "x"), ("z", "x", "y"), ("x", "y", "z"), ("y", "z", "x"))
PARTS = ((0, 1280, ("x", "y", "z")), (1280, 1152, ("y", "z", "x")), (2432, 1152, ("z", "x", "y")))


def expert_kernel(
    owner, shard, resall, gain, wrt, w_gate, w_up, w_down, out,
    ag, hid, chosen, wg, wu, wd, acc, mid, ya, yb, yc, r1a, r1b, r1c, t1a, t1b, t1c,
    r2a, r2b, r2c, t2a, t2b, t2c, r3a, r3b, r3c, z16,
    ags, agr, sibs, sibr, wsem, wds, wdr, ms, mr, rs, rr, zs, zr,
):
    n = lax.axis_index("node")
    l = lax.axis_index("local")
    core = n % 2
    at = {"z": n // 2, "y": l // 4, "x": l % 4}
    sib = (at["z"] * 2 + 1 - core, l)

    def peer(axis, p):
        if axis == "z":
            return (p * 2 + core, l)
        if axis == "y":
            return (n, p * 4 + at["x"])
        return (n, at["y"] * 4 + p)

    bar = pltpu.get_barrier_semaphore()
    for a in "xyz":
        for j in range(1, 4):
            pl.semaphore_signal(bar, 1, device_id=peer(a, (at[a] + j) % 4), device_id_type=MESH)
    pl.semaphore_signal(bar, 1, device_id=sib, device_id_type=MESH)

    keep(w_gate, wg, wsem.at[0])
    keep(w_up, wu, wsem.at[1])
    own_cols = pl.ds(pl.multiple_of(core * 3584, 128), 3584)
    sib_cols = pl.ds(pl.multiple_of((1 - core) * 3584, 128), 3584)
    keep(w_down.at[:, own_cols], wd.at[0], wsem.at[2])
    for q in range(4):
        ag[core, q, at["z"], at["y"], at["x"]] = shard[:, q * 128:(q + 1) * 128]
    pl.semaphore_wait(bar, 10)

    everything = pl.ds(0, 4)

    def slab(q, s, val):
        order = GATHER[q]
        idx = []
        for a in "zyx":
            if a in order[:s]:
                idx.append(everything)
            elif a == order[s]:
                idx.append(val)
            else:
                idx.append(at[a])
        return ag.at[core, q, idx[0], idx[1], idx[2]]

    def gather_start(q, s):
        a = GATHER[q][s]
        for j in range(1, 4):
            p = (at[a] + j) % 4
            send(slab(q, s, at[a]), slab(q, s, at[a]), ags.at[q, s, p], agr.at[q, s, at[a]], peer(a, p))

    def gather_wait(q, s):
        a = GATHER[q][s]
        for j in range(1, 4):
            p = (at[a] + j) % 4
            landed(slab(q, s, p), agr.at[q, s, p])

    for q in range(4):
        gather_start(q, 0)
    send(w_down.at[:, sib_cols], wd.at[1], wds, wdr, sib)

    to = iota((128, 128), 0)
    perm = (iota((128, 128), 1) == (to % 16) * 8 + to // 16).astype(BF)

    def unpack(g):
        rows = pl.ds(pl.multiple_of(g * 16, 16), 16)
        r = jnp.dot(perm, resall[pl.ds(g * 8, 8)].reshape(128, 1024), preferred_element_type=F32).astype(BF)
        for k in range(8):
            hid[rows, k * 896:(k + 1) * 896] = r[k * 16:(k + 1) * 16, :896]
        chosen[rows, :] = r[:16, 896:]

    each(0, 4, unpack)
    for s in range(1, 3):
        for q in range(4):
            gather_wait(q, s - 1)
            gather_start(q, s)
        each(4 * s, 4 * s + 4, unpack)
    each(12, 16, unpack)
    for q in range(4):
        gather_wait(q, 2)
        send(ag.at[core, q], ag.at[core, q], sibs.at[q], sibr.at[q], sib)

    row = iota((256, 64), 0)
    req = iota((256, 64), 1)
    own = jnp.broadcast_to(owner[...], (256, 64))
    target, source = own // 16, req // 8
    line = home_local(source, target) * 16 + (source // 2) * 2 + row % 2
    place = jnp.sum(jnp.where(own == row // 2, line + 1, 0), axis=1, keepdims=True) - 1
    pick_lo = (iota((256, 256), 1) == place).astype(BF)
    pick_hi = ((iota((256, 256), 1) == place + 8) & (place >= 0)).astype(BF)

    acc[...] = jnp.zeros_like(acc)
    landed(wg, wsem.at[0])
    landed(wu, wsem.at[1])
    for q in range(4):
        landed(ag.at[1 - core, q], sibr.at[q])

    def block(k, squares):
        z, c = k // 2, k % 2
        low, high = [], []
        for q in (0, 2):
            b = jnp.concatenate(
                [ag[c, q, z].reshape(256, 128), ag[c, q + 1, z].reshape(256, 128)], axis=1
            )
            low.append(jnp.dot(pick_lo, b, preferred_element_type=F32))
            high.append(jnp.dot(pick_hi, b, preferred_element_type=F32))
        attn = jnp.concatenate([low[0], low[1], high[0], high[1][:, :128]], axis=1)
        cols = pl.ds(pl.multiple_of(k * 896, 128), 896)
        h = (hid[:, cols].astype(F32) + attn).astype(BF)
        hid[:, cols] = h
        wide = h.astype(F32)
        hg = (wide * gain[:, cols]).astype(BF)
        rows = pl.ds(pl.multiple_of(k * 896, 128), 896)
        acc[:, :256] += jnp.dot(hg, wg[rows, :], preferred_element_type=F32)
        acc[:, 256:512] += jnp.dot(hg, wu[rows, :], preferred_element_type=F32)
        acc[:, 512:] += lax.dot_general(hg, wrt[:, cols], NT, preferred_element_type=F32)
        return squares + jnp.sum(wide * wide, axis=1, keepdims=True)
    squares = lax.fori_loop(0, 8, block, jnp.zeros((256, 1), F32))
    factor = lax.rsqrt(squares * (1.0 / 7168) + norm_eps)
    gated = acc[:, :256] * factor
    lifted = acc[:, 256:512] * factor
    mid[0] = (gated * jax.nn.sigmoid(gated) * lifted).astype(BF)
    send(mid.at[0], mid.at[1], ms, mr, sib)

    three = acc[:, 512:]
    logits = three[:, :128] + three[:, 128:256] + three[:, 256:]
    affinity = jax.nn.sigmoid(logits * factor)
    picked = jnp.where(chosen[...].astype(F32) > 0.5, affinity, 0.0)
    combine = (picked / jnp.sum(picked, axis=1, keepdims=True) * route_scale).astype(BF)
    lane = iota((256, 128), 1)
    e_own, e_sib = n * 2 + l // 8, sib[0] * 2 + l // 8

    landed(wd.at[0], wsem.at[2])
    landed(wd.at[1], wdr)
    landed(mid.at[1], mr)

    i = iota((256, 256), 0)
    src = iota((256, 256), 1)
    ybuf, r1, t1 = (ya, yb, yc), (r1a, r1b, r1c), (t1a, t1b, t1c)
    r2, t2, r3 = (r2a, r2b, r2c), (t2a, t2b, t2c), (r3a, r3b, r3c)
    for k, (lo, width, order) in enumerate(PARTS):
        digit = {order[0]: i // 64, order[1]: i // 16 % 4, order[2]: i // 4 % 4}
        natural = ((digit["z"] * 2 + i // 2 % 2) * 16 + digit["y"] * 4 + digit["x"]) * 2 + i % 2
        turn = (src == natural).astype(BF)
        m0 = jnp.dot(turn, mid[0], preferred_element_type=F32).astype(BF)
        m1 = jnp.dot(turn, mid[1], preferred_element_type=F32).astype(BF)
        cw = jnp.dot(turn, combine, preferred_element_type=F32)
        w0 = jnp.sum(jnp.where(lane == e_own, cw, 0.0), axis=1, keepdims=True)
        w1 = jnp.sum(jnp.where(lane == e_sib, cw, 0.0), axis=1, keepdims=True)
        for c0 in range(0, width, 384 if width % 384 == 0 else 640):
            cn = 384 if width % 384 == 0 else 640
            a = jnp.dot(m0, wd[0, :, lo + c0:lo + c0 + cn], preferred_element_type=F32) * w0
            b = jnp.dot(m1, wd[1, :, lo + c0:lo + c0 + cn], preferred_element_type=F32) * w1
            ybuf[k][:, :, c0:c0 + cn] = (a + b).astype(BF).reshape(4, 64, cn)
        a1 = order[0]
        for j in range(1, 4):
            p = (at[a1] + j) % 4
            send(ybuf[k].at[p], r1[k].at[at[a1]], rs.at[k, 0, p], rr.at[k, 0, at[a1]], peer(a1, p))
    for k, (lo, width, order) in enumerate(PARTS):
        a1, a2 = order[0], order[1]
        tot = ybuf[k][at[a1]].astype(F32)
        for j in range(1, 4):
            p = (at[a1] + j) % 4
            landed(r1[k].at[p], rr.at[k, 0, p])
            tot = tot + r1[k][p].astype(F32)
        t1[k][...] = tot.astype(BF).reshape(4, 16, width)
        for j in range(1, 4):
            p = (at[a2] + j) % 4
            send(t1[k].at[p], r2[k].at[at[a2]], rs.at[k, 1, p], rr.at[k, 1, at[a2]], peer(a2, p))
    for k, (lo, width, order) in enumerate(PARTS):
        a2, a3 = order[1], order[2]
        tot = t1[k][at[a2]].astype(F32)
        for j in range(1, 4):
            p = (at[a2] + j) % 4
            landed(r2[k].at[p], rr.at[k, 1, p])
            tot = tot + r2[k][p].astype(F32)
        t2[k][...] = tot.astype(BF)
        for j in range(1, 4):
            p = (at[a3] + j) % 4
            send(t2[k], r3[k].at[at[a3]], rs.at[k, 2, p], rr.at[k, 2, at[a3]], peer(a3, p))
    for k, (lo, width, order) in enumerate(PARTS):
        a3 = order[2]
        tot = t2[k][...].astype(F32)
        for j in range(1, 4):
            p = (at[a3] + j) % 4
            landed(r3[k].at[p], rr.at[k, 2, p])
            tot = tot + r3[k][p].astype(F32)
        z16[core, :, lo:lo + width] = tot.astype(BF)
    send(z16.at[core], z16.at[core], zs, zr, sib)
    landed(z16.at[1 - core], zr)

    up, dn = iota((16, 16), 0), iota((16, 16), 1)
    s = n * 16 + l
    sel = ((up < 2) & (dn == (s % 8) * 2 + up)).astype(BF)
    rows = pl.ds(pl.multiple_of(s // 8 * 16, 16), 16)
    for half in range(2):
        for k, (lo, width, order) in enumerate(PARTS):
            c0 = half * 3584 + lo
            base = jnp.dot(sel, hid[rows, c0:c0 + width], preferred_element_type=F32)
            pickz = ((up < 2) & (dn == at[order[2]] * 4 + core * 2 + up)).astype(BF)
            mix = jnp.dot(pickz, z16[half, :, lo:lo + width], preferred_element_type=F32)
            out[:, c0:c0 + width] = (base + mix)[:2].astype(BF)

    for q in range(4):
        for s in range(3):
            a = GATHER[q][s]
            for j in range(1, 4):
                p = (at[a] + j) % 4
                landed(slab(q, s, at[a]), ags.at[q, s, p])
        landed(ag.at[core, q], sibs.at[q])
    landed(wd.at[1], wds)
    landed(mid.at[0], ms)
    landed(z16.at[core], zs)
    for k, (lo, width, order) in enumerate(PARTS):
        for s, buf in enumerate((ybuf[k], t1[k], t2[k])):
            for j in range(1, 4):
                p = (at[order[s]] + j) % 4
                landed(buf if s == 2 else buf.at[p], rs.at[k, s, p])


def experts(owner, shard, resall, gain, wrt, w_gate, w_up, w_down):
    dma = pltpu.SemaphoreType.DMA
    vm = pl.BlockSpec(memory_space=pltpu.VMEM)
    anywhere = pl.BlockSpec(memory_space=pl.ANY)
    widths = [w for _, w, _ in PARTS]
    return pl.pallas_call(
        expert_kernel,
        name="experts",
        out_shape=jax.ShapeDtypeStruct((2, 7168), BF),
        in_specs=[vm, vm, vm, vm, vm, anywhere, anywhere, anywhere],
        out_specs=vm,
        scratch_shapes=[
            pltpu.VMEM((2, 4, 4, 4, 4, 16, 128), BF),
            pltpu.VMEM((256, 7168), BF),
            pltpu.VMEM((256, 128), BF),
            pltpu.VMEM((7168, 256), BF),
            pltpu.VMEM((7168, 256), BF),
            pltpu.VMEM((2, 256, 3584), BF),
            pltpu.VMEM((256, 512 + 384), F32),
            pltpu.VMEM((2, 256, 256), BF),
        ]
        + [pltpu.VMEM((4, 64, w), BF) for w in widths]
        + [pltpu.VMEM((4, 64, w), BF) for w in widths]
        + [pltpu.VMEM((4, 16, w), BF) for w in widths]
        + [pltpu.VMEM((4, 16, w), BF) for w in widths]
        + [pltpu.VMEM((16, w), BF) for w in widths]
        + [pltpu.VMEM((4, 16, w), BF) for w in widths]
        + [
            pltpu.VMEM((2, 16, 3584), BF),
            dma((4, 3, 4)), dma((4, 3, 4)), dma((4,)), dma((4,)), dma((3,)),
            dma, dma, dma, dma, dma((3, 3, 4)), dma((3, 3, 4)), dma, dma,
        ],
        compiler_params=pltpu.CompilerParams(
            collective_id=1, has_side_effects=True, vmem_limit_bytes=56 << 20
        ),
    )(owner, shard, resall, gain, wrt, w_gate, w_up, w_down)


def shards(
    latent_cache, lengths, owner_map, queries, new_latent, residual, w_value, w_out,
    norm_gain, w_router, expert_ids, w_gate, w_up, w_down,
):
    q = queries.reshape(2, 128, 576).transpose(1, 0, 2).reshape(16, 16, 576)
    spare = jnp.pad(new_latent.reshape(2, 9, 64), ((0, 14), (0, 7), (0, 0)))
    qc = jnp.concatenate([q, spare], axis=2)
    chosen = (expert_ids[0][:, :, None] == jnp.arange(128, dtype=jnp.int32)).any(axis=1)
    marks = jnp.pad(chosen.astype(BF)[:, None, :], ((0, 0), (0, 7), (0, 0)))
    res = jnp.concatenate([residual.reshape(2, 8, 896), marks], axis=2).reshape(16, 1024)
    resall = lax.all_gather(res, ("node", "local"), axis=0, tiled=False)
    wt = w_router.T
    hi = lax.reduce_precision(wt, 8, 7)
    mi = lax.reduce_precision(wt - hi, 8, 7)
    lo = wt - hi - mi
    wrt = jnp.pad(jnp.stack([hi, mi, lo]), ((0, 0), (0, 112), (0, 0))).reshape(384, 7168).astype(BF)
    shard = attend(owner_map, lengths, latent_cache, qc, w_value[0], w_out)
    out = experts(
        owner_map[None, :], shard, resall, norm_gain[None, :], wrt, w_gate, w_up, w_down
    )
    return out[None]


def solution(mesh):
    both = ("node", "local")
    in_specs = (
        P("node", None, "local"), P(), P(), P(both, None, None), P(both, None, None),
        P(both, None, None), P(both, None, None), P(both, None), P(), P(),
        P(both, None, None), P(None, both), P(None, both), P(both, None),
    )
    return jax.shard_map(
        shards, mesh=mesh, in_specs=in_specs, out_specs=P(both, None, None), check_vma=False
    )
```

time: 455 us -> 157 us (0.35)
  waiting for transfers between devices: 255 us -> 3.72 us
  Pallas kernels: 0 us -> 125 us
  blocking collectives: 68.6 us -> 0 us
  local copies, waits for them, and re-layouts: 44.3 us -> 10.4 us
  starting transfers between devices: 25.9 us -> 0.01 us
  matrix products: 25.7 us -> 0 us
  other arithmetic: 17.8 us -> 4.64 us
    unnamed x2 -> x1, waiting for transfers between devices: 156 us -> 0.02 us
    pallas_call x0 -> x2, Pallas kernels: none -> 125 us  [the longest x1 72.8 us: attend(): pl.pallas_call(attend_kernel, name='attend', out_shape=jax.ShapeDtypeStru...]
    all_to_all x4 -> x0, waiting for transfers between devices: 99 us -> none  [the longest x1 46 us: shards(): lax.all_to_all(spread, ('node', 'local'), split_axis=0, concat_axis=0, ti...]
    all_to_all x2 -> x0, blocking collectives: 68.6 us -> none  [the longest x1 51.3 us: shards(): lax.all_to_all(partial_value.astype(jnp.bfloat16), ('node', 'local'), spl...]
    all_to_all x4 -> x0, starting transfers between devices: 25.8 us -> none  [the longest x1 6.93 us: shards(): lax.all_to_all(sectioned, 'local', split_axis=0, concat_axis=2, tiled=True)]
    dot_general x9 -> x0, matrix products: 25.7 us -> none  [the longest x1 11.2 us: expert_rows(): return jnp.dot(middle, down_part, preferred_element_type=jnp.float32)]
    reshape x3, local copies, waits for them, and re-layouts: 17.7 us -> 2.3 us  [the longest x2 1.53 us: shards(): q = queries.reshape(2, 128, 576).transpose(1, 0, 2).reshape(16, 16, 576)]
    convert_element_type x2 -> x0, other arithmetic: 8.05 us -> none  [the longest x1 7.95 us: shards(): partial_value.astype(jnp.bfloat16)]
  transfers between devices with their start and end apart: 5 -> 1, of which waited for: 5 -> 1; matrix products, arithmetic and copies ran while one was open for 1% -> 4% of each run, Pallas kernels for 0% -> 46%
where the time goes in v1:
time: 157 us
  Pallas kernels  125 us (80%)
  between operations  13.5 us (9%)
  local copies, waits for them, and re-layouts  10.4 us (7%)
  other arithmetic  4.64 us (3%)
  waiting for transfers between devices  3.72 us (2%)
    pallas_call x1, Pallas kernels, attend(): pl.pallas_call(attend_kernel, name='attend', out_shape=jax.ShapeDtypeStru...  72.8 us
    pallas_call x1, Pallas kernels, experts(): pl.pallas_call(expert_kernel, name='experts', out_shape=jax.ShapeDtypeStr...  52 us
    unnamed x15, local copies, waits for them, and re-layouts  6.96 us
    all_gather x1, waiting for transfers between devices, shards(): resall = lax.all_gather(res, ('node', 'local'), axis=0, tiled=False)  3.7 us
    another operation x2, other arithmetic, shards(): jnp.stack([hi, mi, lo])  3.16 us
  transfers between devices with their start and end apart: 1, of which 1 were waited for; matrix products, arithmetic and copies ran while one was open for 4% of the time, Pallas kernels for 46%

profile of v1, /device:TPU:1, one launch (start us, length us, event | category | flops | bytes accessed | tf_op | source)
XLA Modules:
  0.0 157.1 jit_solution(6845828196491169628)
XLA Ops:
  6.5 0.0 all-gather.2.cloned.1.call-start
  6.5 0.8 concatenate.14
  7.4 0.8 fusion.11
  8.2 0.6 pad_maximum_fusion
  8.8 0.0 all-gather.2.cloned.1.call-update
  8.8 1.3 reshape.26
  10.1 0.3 copy.21
  10.4 0.2 reshape.27
  10.7 0.8 reshape.28
  11.5 0.1 fusion.7.qc
  11.5 1.5 copy-done
  13.0 1.3 copy-done.1
  14.3 0.9 copy-done.2
  15.2 0.7 copy-done.4
  15.9 0.7 copy-done.5
  16.5 72.8 %attend.1.shard = bf16[16,512]{1,0:T(8,128)(2,1)S(1)} custom-call(s32[64]{0:T(128)S(1)} %copy-done.4, s32[64]{0:T(128)S(1)} %copy-done.5, bf16[8,576,128]{2,1,0:T(8,128)(2,1)S(1)} %copy-done.1, bf16[16,16,640]{2,1,0:T(8,128)(2,1)S(1)} %fusion.7.qc, bf16[512,128]{1,0:T(8,128)(2,1)S(1)} %bitcast.30, bf16[128,7168]{1,0:T(8,128)(2,1)S(1)} %copy-done), custom_call_target="tpu_custom_call" | custom-call | tf_op jit(solution)/shard_map/attend/pallas_call | solution.py:244
  89.3 0.0 copy-start.3
  89.3 0.6 copy-done.3
  89.9 0.0 copy-done.6
  89.9 0.1 fusion.9
  90.0 3.1 %fusion.4 = bf16[3,128,7168]{2,1,0:T(8,128)(2,1)} fusion(bf16[1,16,7168]{2,1,0:T(8,128)(2,1)S(1)} %get-tuple-element.6, bf16[1,16,7168]{2,1,0:T(8,128)(2,1)S(1)} %get-tuple-element.7, bf16[1,16,7168]{2,1,0:T(8,128)(2,1)S(1)} %get-tuple-element.5), kind=kLoop, calls=%fused_computation.5 | loop fusion | flops 27525120 | bytes 6193152 | tf_op jit(solution)/shard_map/stack | solution.py:555
  93.1 3.7 %all-gather.2.cloned.1.call-done.resall = bf16[128,16,1024]{2,1,0:T(8,128)(2,1)} async-done(((bf16[1,16,1024]{2,1,0:T(8,128)(2,1)}), bf16[128,16,1024]{2,1,0:T(8,128)(2,1)}) %all-gather.2.cloned.1.call-update) | async-done | bytes 4194320 | tf_op jit(solution)/shard_map/all_gather | solution.py:550
  96.8 52.0 %experts.1 = bf16[2,7168]{1,0:T(2,128)(2,1)} custom-call(s32[1,64]{1,0:T(1,128)} %bitcast.31, bf16[16,512]{1,0:T(8,128)(2,1)} %copy-done.3, bf16[128,16,1024]{2,1,0:T(8,128)(2,1)} %all-gather.2.cloned.1.call-done.resall, f32[1,7168]{1,0:T(1,128)} %bitcast.35, bf16[384,7168]{1,0:T(8,128)(2,1)} %bitcast.32, bf16[7168,256]{1,0:T(8,128)(2,1)} %w_gate.1, ...), custom_call_target="tpu_custom_call" | custom-call | tf_op jit(solution)/shard_map/experts/pallas_call | solution.py:507
  148.8 1.4 copy.26
  (8 shorter events, 0.0 us)
Async XLA Ops:
  6.5 83.4 %copy-start.6 = (f32[7168,16]{0,1:T(8,128)S(1)}, f32[7168,16]{0,1:T(8,128)}, u32[]{:S(2)}) copy-start(f32[7168,16]{0,1:T(8,128)} %param.23) | copy-start | bytes 1376260
  6.5 90.3 %all-gather.2.cloned.1.call-start = ((), (), s32[]{:S(2)}) async-start(), calls=%async_computation | async-start | bytes 4227072 | tf_op jit(solution)/shard_map/all_gather | solution.py:550
  11.5 1.5 copy-start
  13.0 1.3 copy-start.1
  14.3 0.9 copy-start.2
  15.2 0.7 copy-start.4
  15.9 0.7 copy-start.5
  89.3 0.6 copy-start.3
Sparse Core Ops, SparseCore 0:
  10.5 86.2 all-gather.1

commit v2 on v1

v2 whole, which is shorter than its diff:
```python
import functools

import jax
import jax.numpy as jnp
from jax import lax
from jax.experimental import pallas as pl
from jax.experimental.pallas import tpu as pltpu
from jax.sharding import PartitionSpec as P

MESH = pl.DeviceIdType.MESH
BF = jnp.bfloat16
F32 = jnp.float32
score_scale = 192.0 ** (-0.5)
route_scale = 2.5
norm_eps = 1e-06
NT = (((1,), (1,)), ((), ()))


def iota(shape, dim):
    return lax.broadcasted_iota(jnp.int32, shape, dim)


def landed(ref, sem):
    pltpu.make_async_copy(ref, ref, sem).wait()


def send(src, dst, send_sem, recv_sem, device):
    pltpu.make_async_remote_copy(
        src_ref=src, dst_ref=dst, send_sem=send_sem, recv_sem=recv_sem,
        device_id=device, device_id_type=MESH,
    ).start()


def keep(src, dst, sem):
    pltpu.make_async_copy(src, dst, sem).start()


def home_local(node, target):
    row = target // 2
    return row * 4 + (target % 2) * 2 + (row + node) % 2


def each(lo, hi, body):
    def step(i, carry):
        body(i)
        return carry
    lax.fori_loop(lo, hi, step, 0)


GATHER = (("y", "z", "x"), ("z", "x", "y"), ("x", "y", "z"), ("y", "z", "x"))
PARTS = ((0, 1280, ("x", "y", "z")), (1280, 1152, ("y", "z", "x")), (2432, 1152, ("z", "x", "y")))
WIDTHS = tuple(w for _, w, _ in PARTS)


def row_of(owner, s, t):
    own = jnp.broadcast_to(owner, s.shape)
    served = (iota(s.shape, 1) // 8) * 16 + (own // 16) * 2 + t + 1
    found = jnp.sum(jnp.where(own == s, served, 0), axis=1, keepdims=True)
    below = jnp.sum(jnp.where(own < s, 1, 0), axis=1, keepdims=True)
    return jnp.where(found > 0, found - 1, 128 + (s[:, :1] - below) * 2 + t[:, :1])


def kernel(
    owner, lengths, ids, owner_row, qc, fresh, res, gain, router, cache, w_value, w_out, w_gate, w_up, w_down, out,
    cv, csend, crecv, qs, q1, q2s, q3, sbuf, acc, att, c1, wvr, wr, hv, hvr, ys, yr,
    rtile, rg, ag, nat, hid, marks, chosen, wg, wu, wd, wrt, facc, mid, turns,
    ya, yb, yc, r1a, r1b, r1c, t1a, t1b, t1c, r2a, r2b, r2c, t2a, t2b, t2c, r3a, r3b, r3c, z16,
    ld, cs, cr, q1ss, q1r, q2ss, q3r, a1s, a1r, vs, vr, ws, wrr, hs, hr, yss, yrr,
    rgs, rgr, rbs, rbr, ags, agr, abs_, abr, wds, wdr, ms, mr, rs, rr, zs, zr,
):
    n = lax.axis_index("node")
    l = lax.axis_index("local")
    core = n % 2
    at = {"z": n // 2, "y": l // 4, "x": l % 4}
    sib = (at["z"] * 2 + 1 - core, l)
    is_home = (at["x"] + at["y"]) % 2 == core
    mine = at["y"] * 2 + at["x"] // 2

    keep(cache, cv, ld.at[0])
    bar = pltpu.get_barrier_semaphore()

    def hello(device):
        pl.semaphore_signal(bar, 1, device_id=device, device_id_type=MESH)
    each(1, 16, lambda j: hello((n, (l + j) % 16)))
    each(1, 8, lambda j: hello(((n + j) % 8, l)))

    @pl.when(is_home & (mine != n))
    def _():
        each(0, 16, lambda j: hello((mine, j)))
    keep(w_value, wvr.at[n], vr.at[n])
    keep(w_out.at[:, pl.ds(pl.multiple_of(n * 896, 128), 896)], wr.at[n], wrr.at[n])
    keep(w_gate, wg, ld.at[1])
    keep(w_up, wu, ld.at[2])
    own_cols = pl.ds(pl.multiple_of(core * 3584, 128), 3584)
    sib_cols = pl.ds(pl.multiple_of((1 - core) * 3584, 128), 3584)
    keep(w_down.at[:, own_cols], wd.at[0], ld.at[3])

    qs[:, :, :576] = qc[...]
    qs[:, :, 576:] = jnp.zeros((16, 16, 64), BF)
    own_band = iota((16, 576), 1) // 64 == iota((16, 576), 0)
    fold = (iota((576, 64), 0) % 64 == iota((576, 64), 1)).astype(BF)
    new = fresh[...].astype(F32)
    for t in range(2):
        bands = jnp.where(own_band, jnp.broadcast_to(new[t:t + 1], (16, 576)), 0.0).astype(BF)
        qs[t, :, 576:640] = jnp.dot(bands, fold, preferred_element_type=F32).astype(BF)
    landed(cv, ld.at[0])
    pl.semaphore_wait(bar, 29)

    keep(qs.at[l], q1.at[l], q1r.at[l])

    def q_first(j):
        p = (l + j) % 16
        send(qs.at[p], q1.at[l], q1ss.at[p], q1r.at[l], (n, p))
    each(1, 16, q_first)

    def cache_send(j):
        t = (l + j) % 8
        pick = jnp.int32(0)
        for i in range(8):
            pick = jnp.where(owner[n * 8 + i] // 16 == t, i, pick)
        csend[t] = cv[pick]
        dest = home_local(n, t)

        @pl.when(dest == l)
        def _():
            keep(csend.at[t], crecv.at[l], cr.at[l])

        @pl.when(dest != l)
        def _():
            send(csend.at[t], crecv.at[l], cs.at[t], cr.at[l], (n, dest))
    each(0, 8, cache_send)

    def v_send(j):
        p = (n + j) % 8
        send(w_value, wvr.at[n], vs.at[p], vr.at[n], (p, l))
    each(1, 8, v_send)

    each(0, 16, lambda j: landed(q1.at[j], q1r.at[j]))

    def q_second(j):
        p = (n + j) % 8
        pick = jnp.int32(0)
        for i in range(8):
            o = owner[p * 8 + i]
            pick = jnp.where(o // 16 == n, o % 16, pick)
        q2s[p] = q1[pick]
        dest = home_local(p, n)
        self_ = (p == n) & (dest == l)

        @pl.when(self_)
        def _():
            keep(q2s.at[p], q3.at[l], q3r.at[l])

        @pl.when(jnp.logical_not(self_))
        def _():
            send(q2s.at[p], q3.at[l], q2ss.at[p], q3r.at[l], (p, dest))
    each(0, 8, q_second)

    def w_send(j):
        p = (n + j) % 8
        send(w_out.at[:, pl.ds(pl.multiple_of(p * 896, 128), 896)], wr.at[n], ws.at[p], wrr.at[n], (p, l))
    each(1, 8, w_send)
    send(w_down.at[:, sib_cols], wd.at[1], wds, wdr, sib)

    everything = pl.ds(0, 4)

    def peer(axis, p):
        if axis == "z":
            return (p * 2 + core, l)
        if axis == "y":
            return (n, p * 4 + at["x"])
        return (n, at["y"] * 4 + p)

    def slab(buf, q, s, val):
        order = GATHER[q]
        idx = []
        for a in "zyx":
            if a in order[:s]:
                idx.append(everything)
            elif a == order[s]:
                idx.append(val)
            else:
                idx.append(at[a])
        return buf.at[core, q, idx[0], idx[1], idx[2]]

    def gather_start(buf, ss, rs_, q, s):
        a = GATHER[q][s]
        for j in range(1, 4):
            p = (at[a] + j) % 4
            send(slab(buf, q, s, at[a]), slab(buf, q, s, at[a]), ss.at[q, s, p], rs_.at[q, s, at[a]], peer(a, p))

    def gather_wait(buf, rs_, q, s):
        a = GATHER[q][s]
        for j in range(1, 4):
            p = (at[a] + j) % 4
            landed(slab(buf, q, s, p), rs_.at[q, s, p])

    def gather_drain(buf, ss):
        for q in range(4):
            for s in range(3):
                a = GATHER[q][s]
                for j in range(1, 4):
                    p = (at[a] + j) % 4
                    landed(slab(buf, q, s, at[a]), ss.at[q, s, p])

    r = res[...].astype(F32)
    line = iota((16, 896), 0)
    tile = jnp.zeros((16, 896), F32)
    mark = jnp.zeros((16, 128), F32)
    for t in range(2):
        for k in range(8):
            tile = jnp.where(line == t * 8 + k, jnp.broadcast_to(r[t:t + 1, k * 896:(k + 1) * 896], (16, 896)), tile)
        hit = iota((16, 128), 1) == ids[t, 0]
        for j in range(1, 8):
            hit = hit | (iota((16, 128), 1) == ids[t, j])
        mark = jnp.where(hit & (iota((16, 128), 0) == t * 8), 1.0, mark)
    rtile[...] = jnp.concatenate([tile, mark], axis=1).astype(BF)
    for q in range(4):
        rg[core, q, at["z"], at["y"], at["x"]] = rtile[:, q * 256:(q + 1) * 256]
        gather_start(rg, rgs, rgr, q, 0)

    wt = router[...]
    hi = wt.astype(BF)
    rest = wt - hi.astype(F32)
    mi = rest.astype(BF)
    wrt[0:16, :] = hi
    wrt[16:32, :] = mi
    wrt[32:48, :] = (rest - mi.astype(F32)).astype(BF)
    wrt[48:128, :] = jnp.zeros((80, 7168), BF)

    i64 = iota((256, 64), 0)
    spot = row_of(owner_row[...], i64 // 2, i64 % 2)
    to_nat = jnp.where(iota((256, 256), 1) == spot, 1.0, 0.0)
    turns[3] = to_nat.T.astype(BF)
    for k, (lo, width, order) in enumerate(PARTS):
        digit = {order[0]: i64 // 64, order[1]: i64 // 16 % 4, order[2]: i64 // 4 % 4}
        s64 = (digit["z"] * 2 + i64 // 2 % 2) * 16 + digit["y"] * 4 + digit["x"]
        turns[k] = (iota((256, 256), 1) == row_of(owner_row[...], s64, i64 % 2)).astype(BF)

    for q in range(4):
        gather_wait(rg, rgr, q, 0)
        gather_start(rg, rgs, rgr, q, 1)

    @pl.when(is_home)
    def _():
        each(0, 16, lambda j: landed(q3.at[j], q3r.at[j]))
        length = jnp.int32(0)
        for i in range(8):
            r = n * 8 + i
            length = jnp.where(owner[r] // 16 == mine, lengths[r], length)
        q = q3[...].reshape(256, 640)[:, :576]
        spread = (iota((64, 576), 1) % 64 == iota((64, 576), 0)).astype(BF)
        rows = []
        for t in range(2):
            wide = jnp.dot(q3[t][:, 576:640], spread, preferred_element_type=F32)
            rows.append(jnp.sum(jnp.where(own_band, wide, 0.0), axis=0, keepdims=True))
        up = iota((128, 576), 0)
        fresh_rows = jnp.where(up == 0, rows[0], jnp.where(up == 1, rows[1], 0.0)).astype(BF)
        fs = lax.dot_general(q, fresh_rows, NT, preferred_element_type=F32) * score_scale
        fs = jnp.where(iota((256, 128), 1) <= iota((256, 128), 0) % 2, fs, -jnp.inf)

        def score(p, top):
            landed(crecv.at[2 * p], cr.at[2 * p])
            landed(crecv.at[2 * p + 1], cr.at[2 * p + 1])
            keys = jnp.concatenate([crecv[2 * p], crecv[2 * p + 1]], axis=1)
            s = jnp.dot(q, keys, preferred_element_type=F32) * score_scale
            s = jnp.where(p * 256 + iota((256, 256), 1) < length, s, -jnp.inf)
            sbuf[p] = s
            return jnp.maximum(top, jnp.max(s, axis=1, keepdims=True))
        top = lax.fori_loop(0, 8, score, jnp.max(fs, axis=1, keepdims=True))
        fe = jnp.exp(fs - top)
        acc[...] = jnp.dot(fe.astype(BF), fresh_rows[:, :512], preferred_element_type=F32)

        def weigh(p, total):
            e = jnp.exp(sbuf[p] - top)
            values = jnp.concatenate([crecv[2 * p, :512, :], crecv[2 * p + 1, :512, :]], axis=1)
            acc[...] += lax.dot_general(e.astype(BF), values, NT, preferred_element_type=F32)
            return total + jnp.sum(e, axis=1, keepdims=True)
        total = lax.fori_loop(0, 8, weigh, jnp.sum(fe, axis=1, keepdims=True))
        att[...] = (acc[...] / total).astype(BF).reshape(16, 16, 512)

        keep(att.at[l], c1.at[mine], a1r.at[mine])

        def head_local(j):
            p = (l + j) % 16
            send(att.at[p], c1.at[mine], a1s.at[p], a1r.at[mine], (n, p))
        each(1, 16, head_local)

    for q in range(4):
        gather_wait(rg, rgr, q, 1)
        gather_start(rg, rgs, rgr, q, 2)

    each(0, 8, lambda j: landed(wvr.at[j], vr.at[j]))
    each(0, 8, lambda j: landed(c1.at[j], a1r.at[j]))
    to = iota((128, 128), 0)
    perm = (iota((128, 128), 1) == (to // 2 % 8) * 16 + (to // 16) * 2 + to % 2).astype(BF)
    by_head = jnp.dot(perm, c1[...].reshape(128, 512), preferred_element_type=F32).astype(BF)
    for k in range(8):
        hv[:, k * 128:(k + 1) * 128] = jnp.dot(
            by_head[k * 16:(k + 1) * 16], wvr[k], preferred_element_type=F32
        ).astype(BF)
    keep(hv, hvr.at[n], hr.at[n])

    def values_out(j):
        p = (n + j) % 8
        send(hv, hvr.at[n], hs.at[p], hr.at[n], (p, l))
    each(1, 8, values_out)
    each(0, 8, lambda j: landed(wr.at[j], wrr.at[j]))
    each(0, 8, lambda j: landed(hvr.at[j], hr.at[j]))
    proj = jnp.dot(
        hvr[...].reshape(128, 1024), wr[...].reshape(1024, 896), preferred_element_type=F32
    ).reshape(16, 8, 896)
    high = jnp.concatenate([proj[:, :, 512:], jnp.zeros((16, 8, 128), F32)], axis=2)
    ys[...] = jnp.concatenate([proj[:, :, :512], high], axis=1).astype(BF)
    keep(ys.at[l], yr.at[l], yrr.at[l])

    def rows_out(j):
        p = (l + j) % 16
        send(ys.at[p], yr.at[l], yss.at[p], yrr.at[l], (n, p))
    each(1, 16, rows_out)
    for q in range(4):
        gather_wait(rg, rgr, q, 2)
        send(rg.at[core, q], rg.at[core, q], rbs.at[q], rbr.at[q], sib)
    each(0, 16, lambda j: landed(yr.at[j], yrr.at[j]))
    tot = yr[0].astype(F32)
    for j in range(1, 16):
        tot = tot + yr[j].astype(F32)
    shard = tot.astype(BF)
    for q in range(4):
        ag[core, q, at["z"], at["y"], at["x"]] = shard[:, q * 128:(q + 1) * 128]
        gather_start(ag, ags, agr, q, 0)

    for q in range(4):
        landed(rg.at[1 - core, q], rbr.at[q])
    deal = (iota((128, 128), 1) == (to % 16) * 8 + to // 16).astype(BF)

    def unpack(g):
        rows = pl.ds(pl.multiple_of(g * 16, 16), 16)
        z, c, y2 = g // 4, g // 2 % 2, g % 2
        x = jnp.concatenate(
            [rg[c, q, z, pl.ds(y2 * 2, 2)].reshape(128, 256) for q in range(4)], axis=1
        )
        d = jnp.dot(deal, x, preferred_element_type=F32).astype(BF)
        for k in range(8):
            nat[rows, k * 896:(k + 1) * 896] = d[k * 16:(k + 1) * 16, :896]
        marks[rows, :] = d[:16, 896:]

    def reorder(k):
        cols = pl.ds(pl.multiple_of(k * 896, 128), 896)
        hid[:, cols] = jnp.dot(turns[3], nat[:, cols], preferred_element_type=F32).astype(BF)

    each(0, 8, unpack)
    for q in range(4):
        gather_wait(ag, agr, q, 0)
        gather_start(ag, ags, agr, q, 1)
    each(8, 16, unpack)
    for q in range(4):
        gather_wait(ag, agr, q, 1)
        gather_start(ag, ags, agr, q, 2)
    each(0, 8, reorder)
    chosen[...] = jnp.dot(turns[3], marks[...], preferred_element_type=F32)
    facc[...] = jnp.zeros_like(facc)
    landed(wg, ld.at[1])
    landed(wu, ld.at[2])
    for q in range(4):
        gather_wait(ag, agr, q, 2)
        send(ag.at[core, q], ag.at[core, q], abs_.at[q], abr.at[q], sib)
    for q in range(4):
        landed(ag.at[1 - core, q], abr.at[q])

    def block(k, squares):
        z, c = k // 2, k % 2
        tops, lows = [], []
        for q in range(4):
            b = ag[c, q, z].reshape(16, 16, 128).astype(F32)
            tops.append(b[:, :8].reshape(128, 128))
            lows.append(b[:, 8:].reshape(128, 128))
        attn = jnp.concatenate(tops + lows[:3], axis=1)
        cols = pl.ds(pl.multiple_of(k * 896, 128), 896)
        wide = hid[:, cols].astype(F32)
        h = jnp.concatenate([wide[:128] + attn, wide[128:]], axis=0).astype(BF)
        hid[:, cols] = h
        wide = h.astype(F32)
        hg = (wide * gain[:, cols]).astype(BF)
        rows = pl.ds(pl.multiple_of(k * 896, 128), 896)
        facc[:, :256] += jnp.dot(hg, wg[rows, :], preferred_element_type=F32)
        facc[:, 256:512] += jnp.dot(hg, wu[rows, :], preferred_element_type=F32)
        facc[:, 512:] += lax.dot_general(hg, wrt[:, cols], NT, preferred_element_type=F32)
        return squares + jnp.sum(wide * wide, axis=1, keepdims=True)
    squares = lax.fori_loop(0, 8, block, jnp.zeros((256, 1), F32))
    factor = lax.rsqrt(squares * (1.0 / 7168) + norm_eps)
    gated = facc[:, :256] * factor
    lifted = facc[:, 256:512] * factor
    mid[0] = (gated * jax.nn.sigmoid(gated) * lifted).astype(BF)
    send(mid.at[0], mid.at[1], ms, mr, sib)

    three = facc[:, 512:]
    logits = three + pltpu.roll(three, 112, 1) + pltpu.roll(three, 96, 1)
    affinity = jax.nn.sigmoid(logits * factor)
    picked = jnp.where(chosen[...] > 0.5, affinity, 0.0)
    combine = (picked / jnp.sum(picked, axis=1, keepdims=True) * route_scale).astype(BF)
    lane = iota((256, 128), 1)
    e_own, e_sib = n * 2 + l // 8, sib[0] * 2 + l // 8
    landed(wd.at[0], ld.at[3])
    landed(wd.at[1], wdr)
    landed(mid.at[1], mr)

    ybuf, r1, t1 = (ya, yb, yc), (r1a, r1b, r1c), (t1a, t1b, t1c)
    r2, t2, r3 = (r2a, r2b, r2c), (t2a, t2b, t2c), (r3a, r3b, r3c)
    for k, (lo, width, order) in enumerate(PARTS):
        m0 = jnp.dot(turns[k], mid[0], preferred_element_type=F32).astype(BF)
        m1 = jnp.dot(turns[k], mid[1], preferred_element_type=F32).astype(BF)
        cw = jnp.dot(turns[k], combine, preferred_element_type=F32)
        w0 = jnp.sum(jnp.where(lane == e_own, cw, 0.0), axis=1, keepdims=True)
        w1 = jnp.sum(jnp.where(lane == e_sib, cw, 0.0), axis=1, keepdims=True)
        cn = 384 if width % 384 == 0 else 640
        for c0 in range(0, width, cn):
            a = jnp.dot(m0, wd[0, :, lo + c0:lo + c0 + cn], preferred_element_type=F32) * w0
            b = jnp.dot(m1, wd[1, :, lo + c0:lo + c0 + cn], preferred_element_type=F32) * w1
            ybuf[k][:, :, c0:c0 + cn] = (a + b).astype(BF).reshape(4, 64, cn)
        a1 = order[0]
        for j in range(1, 4):
            p = (at[a1] + j) % 4
            send(ybuf[k].at[p], r1[k].at[at[a1]], rs.at[k, 0, p], rr.at[k, 0, at[a1]], peer(a1, p))

    s16 = iota((16, 64), 0) * 0 + (n * 16 + l)
    own_rows = row_of(owner_row[...], s16, iota((16, 64), 0) % 2)
    sel = (iota((16, 256), 1) == own_rows).astype(BF)

    for k, (lo, width, order) in enumerate(PARTS):
        a1, a2 = order[0], order[1]
        tot = ybuf[k][at[a1]].astype(F32)
        for j in range(1, 4):
            p = (at[a1] + j) % 4
            landed(r1[k].at[p], rr.at[k, 0, p])
            tot = tot + r1[k][p].astype(F32)
        t1[k][...] = tot.astype(BF).reshape(4, 16, width)
        for j in range(1, 4):
            p = (at[a2] + j) % 4
            send(t1[k].at[p], r2[k].at[at[a2]], rs.at[k, 1, p], rr.at[k, 1, at[a2]], peer(a2, p))
    for k, (lo, width, order) in enumerate(PARTS):
        a2, a3 = order[1], order[2]
        tot = t1[k][at[a2]].astype(F32)
        for j in range(1, 4):
            p = (at[a2] + j) % 4
            landed(r2[k].at[p], rr.at[k, 1, p])
            tot = tot + r2[k][p].astype(F32)
        t2[k][...] = tot.astype(BF)
        for j in range(1, 4):
            p = (at[a3] + j) % 4
            send(t2[k], r3[k].at[at[a3]], rs.at[k, 2, p], rr.at[k, 2, at[a3]], peer(a3, p))
    for k, (lo, width, order) in enumerate(PARTS):
        a3 = order[2]
        tot = t2[k][...].astype(F32)
        for j in range(1, 4):
            p = (at[a3] + j) % 4
            landed(r3[k].at[p], rr.at[k, 2, p])
            tot = tot + r3[k][p].astype(F32)
        z16[core, :, lo:lo + width] = tot.astype(BF)
    send(z16.at[core], z16.at[core], zs, zr, sib)
    landed(z16.at[1 - core], zr)

    up, dn = iota((16, 16), 0), iota((16, 16), 1)
    for half in range(2):
        for k, (lo, width, order) in enumerate(PARTS):
            c0 = half * 3584 + lo
            base = jnp.dot(sel, hid[:, c0:c0 + width], preferred_element_type=F32)
            pickz = ((up < 2) & (dn == at[order[2]] * 4 + core * 2 + up)).astype(BF)
            mix = jnp.dot(pickz, z16[half, :, lo:lo + width], preferred_element_type=F32)
            out[:, c0:c0 + width] = (base + mix)[:2].astype(BF)

    def drain(j):
        p = (l + j) % 16
        landed(qs.at[p], q1ss.at[p])
        landed(ys.at[p], yss.at[p])

        @pl.when(is_home)
        def _():
            landed(att.at[p], a1s.at[p])
    each(1, 16, drain)

    def drain_home(t):
        @pl.when(home_local(n, t) != l)
        def _():
            landed(csend.at[t], cs.at[t])

        @pl.when(jnp.logical_not((t == n) & (home_local(t, n) == l)))
        def _():
            landed(q2s.at[t], q2ss.at[t])
    each(0, 8, drain_home)

    def drain_node(j):
        p = (n + j) % 8
        landed(wvr.at[p], vs.at[p])
        landed(hv, hs.at[p])
        landed(wr.at[p], ws.at[p])
    each(1, 8, drain_node)
    gather_drain(rg, rgs)
    gather_drain(ag, ags)
    for q in range(4):
        landed(rg.at[core, q], rbs.at[q])
        landed(ag.at[core, q], abs_.at[q])
    landed(wd.at[1], wds)
    landed(mid.at[0], ms)
    landed(z16.at[core], zs)
    for k, (lo, width, order) in enumerate(PARTS):
        for s, buf in enumerate((ybuf[k], t1[k], t2[k])):
            for j in range(1, 4):
                p = (at[order[s]] + j) % 4
                landed(buf if s == 2 else buf.at[p], rs.at[k, s, p])


def layer(owner, lengths, ids, qc, fresh, res, gain, router, cache, w_value, w_out, w_gate, w_up, w_down):
    dma = pltpu.SemaphoreType.DMA
    vm = pl.BlockSpec(memory_space=pltpu.VMEM)
    sm = pl.BlockSpec(memory_space=pltpu.SMEM)
    hbm = pl.BlockSpec(memory_space=pl.ANY)
    bf = lambda *shape: pltpu.VMEM(shape, BF)
    f32 = lambda *shape: pltpu.VMEM(shape, F32)
    return pl.pallas_call(
        kernel,
        name="layer",
        out_shape=jax.ShapeDtypeStruct((2, 7168), BF),
        in_specs=[sm, sm, sm, vm, vm, vm, vm, vm, vm, hbm, hbm, hbm, hbm, hbm, hbm],
        out_specs=vm,
        scratch_shapes=[
            bf(8, 576, 128), bf(8, 576, 128), bf(16, 576, 128),
            bf(16, 16, 640), bf(16, 16, 640), bf(8, 16, 640), bf(16, 16, 640),
            f32(8, 256, 256), f32(256, 512), bf(16, 16, 512), bf(8, 16, 512),
            bf(8, 512, 128), bf(8, 128, 896), bf(16, 1024), bf(8, 16, 1024),
            bf(16, 16, 512), bf(16, 16, 512),
            bf(16, 1024), bf(2, 4, 4, 4, 4, 16, 256), bf(2, 4, 4, 4, 4, 16, 128),
            bf(256, 7168), bf(256, 7168), bf(256, 128), f32(256, 128),
            bf(7168, 256), bf(7168, 256), bf(2, 256, 3584), bf(128, 7168),
            f32(256, 640), bf(2, 256, 256), bf(4, 256, 256),
        ]
        + [bf(4, 64, w) for w in WIDTHS] + [bf(4, 64, w) for w in WIDTHS]
        + [bf(4, 16, w) for w in WIDTHS] + [bf(4, 16, w) for w in WIDTHS]
        + [bf(16, w) for w in WIDTHS] + [bf(4, 16, w) for w in WIDTHS]
        + [bf(2, 16, 3584)]
        + [dma((k,)) for k in (4, 8, 16, 16, 16, 8, 16, 16, 8, 8, 8, 8, 8, 8, 8, 16, 16)]
        + [
            dma((4, 3, 4)), dma((4, 3, 4)), dma((4,)), dma((4,)),
            dma((4, 3, 4)), dma((4, 3, 4)), dma((4,)), dma((4,)),
            dma, dma, dma, dma, dma((3, 3, 4)), dma((3, 3, 4)), dma, dma,
        ],
        compiler_params=pltpu.CompilerParams(
            collective_id=0, has_side_effects=True, vmem_limit_bytes=58 << 20
        ),
    )(owner, lengths, ids, owner[None, :], qc, fresh, res, gain, router, cache, w_value, w_out, w_gate, w_up, w_down)


def shards(
    latent_cache, lengths, owner_map, queries, new_latent, residual, w_value, w_out,
    norm_gain, w_router, expert_ids, w_gate, w_up, w_down,
):
    qc = queries.reshape(2, 8, 16, 576).transpose(2, 1, 0, 3).reshape(16, 16, 576)
    out = layer(
        owner_map, lengths, expert_ids[0], qc, new_latent[0], residual[0], norm_gain[None, :], w_router.T,
        latent_cache, w_value[0], w_out, w_gate, w_up, w_down,
    )
    return out[None]


def solution(mesh):
    both = ("node", "local")
    in_specs = (
        P("node", None, "local"), P(), P(), P(both, None, None), P(both, None, None),
        P(both, None, None), P(both, None, None), P(both, None), P(), P(),
        P(both, None, None), P(None, both), P(None, both), P(both, None),
    )
    return jax.shard_map(
        shards, mesh=mesh, in_specs=in_specs, out_specs=P(both, None, None), check_vma=False
    )
```

time: 157 us -> 127 us (0.81)
  between operations: 13.5 us -> 0.02 us
  local copies, waits for them, and re-layouts: 10.4 us -> 3.95 us
  other arithmetic: 4.64 us -> 0 us
  waiting for transfers between devices: 3.72 us -> 0 us
  Pallas kernels: 125 us -> 123 us
    unnamed x15 -> x1, local copies, waits for them, and re-layouts: 6.96 us -> 1.38 us
    all_gather x1 -> x0, waiting for transfers between devices: 3.7 us -> none  [shards(): resall = lax.all_gather(res, ('node', 'local'), axis=0, tiled=False)]
    another operation x2 -> x0, other arithmetic: 3.16 us -> none  [shards(): jnp.stack([hi, mi, lo])]
    pallas_call x2 -> x1, Pallas kernels: 125 us -> 123 us  [layer(): pl.pallas_call(kernel, name='layer', out_shape=jax.ShapeDtypeStruct((2, 7...]
  transfers between devices with their start and end apart: 1 -> 0, of which waited for: 1 -> 0; matrix products, arithmetic and copies ran while one was open for 4% -> 0% of each run, Pallas kernels for 46% -> 0%
where the time goes in v2:
time: 127 us
  Pallas kernels  123 us (97%)
  local copies, waits for them, and re-layouts  3.95 us (3%)
    pallas_call x1, Pallas kernels, layer(): pl.pallas_call(kernel, name='layer', out_shape=jax.ShapeDtypeStruct((2, 7...  123 us
    reshape x3, local copies, waits for them, and re-layouts, shards(): queries.reshape(2, 8, 16, 576).transpose(2, 1, 0, 3).reshape(16, 16, 576)  2.57 us

profile of v2, /device:TPU:1, one launch (start us, length us, event | category | flops | bytes accessed | tf_op | source)
XLA Modules:
  0.0 127.1 jit_solution(17007610296865767134)
XLA Ops:
  0.0 1.3 %reshape.6 = bf16[2,8,16,576]{3,2,1,0:T(8,128)(2,1)S(1)} reshape(bf16[1,2,73728]{2,1,0:T(2,128)(2,1)} %param.17) | data formatting | bytes 589824 | tf_op jit(solution)/shard_map/reshape | solution.py:557
  1.3 0.3 copy.17
  1.6 1.0 reshape.7.qc
  2.6 123.1 %layer.1 = bf16[2,7168]{1,0:T(2,128)(2,1)} custom-call(s32[64]{0:T(128)} %owner.1, s32[64]{0:T(128)} %lengths.1, s32[2,8]{1,0:T(2,128)} %bitcast.19, s32[1,64]{1,0:T(1,128)} %bitcast.18, bf16[16,16,576]{2,1,0:T(8,128)(2,1)} %reshape.7.qc, bf16[2,576]{1,0:T(2,128)(2,1)} %bitcast.17, bf16[2,7168]{1,0:T(2,128)(2,1)} %bitcast.15, f32[1,7168]{1,0:T(1,128)} %bitcast.16, ...), custom_call_target="tpu_custom_call" | custom-call | tf_op jit(solution)/shard_map/layer/pallas_call | solution.py:520
  125.7 1.4 %copy.19 = bf16[1,2,7168]{2,1,0:T(2,128)(2,1)} copy(bf16[1,2,7168]{2,1,0:T(2,128)(2,1)} %bitcast.14) | data formatting | bytes 57344

commit v3 on v2

v3 whole, which is shorter than its diff:
```python
import functools

import jax
import jax.numpy as jnp
from jax import lax
from jax.experimental import pallas as pl
from jax.experimental.pallas import tpu as pltpu
from jax.sharding import PartitionSpec as P

MESH = pl.DeviceIdType.MESH
BF = jnp.bfloat16
F32 = jnp.float32
score_scale = 192.0 ** (-0.5)
route_scale = 2.5
norm_eps = 1e-06
NT = (((1,), (1,)), ((), ()))


def iota(shape, dim):
    return lax.broadcasted_iota(jnp.int32, shape, dim)


def landed(ref, sem):
    pltpu.make_async_copy(ref, ref, sem).wait()


def send(src, dst, send_sem, recv_sem, device):
    pltpu.make_async_remote_copy(
        src_ref=src, dst_ref=dst, send_sem=send_sem, recv_sem=recv_sem,
        device_id=device, device_id_type=MESH,
    ).start()


def keep(src, dst, sem):
    pltpu.make_async_copy(src, dst, sem).start()


def home_local(node, target):
    row = target // 2
    return row * 4 + (target % 2) * 2 + (row + node) % 2


def each(lo, hi, body):
    def step(i, carry):
        body(i)
        return carry
    lax.fori_loop(lo, hi, step, 0)


GATHER = (("y", "z", "x"), ("z", "x", "y"), ("x", "y", "z"), (("y", "z", "x"), ("z", "x", "y")))
RESIDUAL = (("z", "y", "x"), ("z", "x", "y"), ("z", "y", "x"), ("z", "x", "y"))
CACHE_FIRST = 4
RG0_EARLY = 1
V_EARLY = 1
RG1_AT = 1
RG2_AT = (1, 1, 1, 1)
EVEN = ((1, 1), (3, 3), (1, 3), (3, 1), (2, 0), (0, 2), (2, 2), (0, 0))
ODD = ((1, 0), (3, 0), (0, 1), (0, 3), (1, 2), (3, 2), (2, 1), (2, 3))
UNPACK_FIRST = 12
PARTS = ((0, 1280, ("x", "y", "z")), (1280, 1152, ("y", "z", "x")), (2432, 1152, ("z", "x", "y")))
WIDTHS = tuple(w for _, w, _ in PARTS)


def row_of(owner, s, t):
    own = jnp.broadcast_to(owner, s.shape)
    served = (iota(s.shape, 1) // 8) * 16 + (own // 16) * 2 + t + 1
    found = jnp.sum(jnp.where(own == s, served, 0), axis=1, keepdims=True)
    below = jnp.sum(jnp.where(own < s, 1, 0), axis=1, keepdims=True)
    return jnp.where(found > 0, found - 1, 128 + (s[:, :1] - below) * 2 + t[:, :1])


def kernel(
    owner, lengths, ids, owner_hbm, queries_hbm, fresh_hbm, res_hbm, gain_hbm, router_hbm, cache, w_value, w_out, w_gate, w_up, w_down, out,
    owner_row, queries, fresh, res, gain, router, cv, csend, crecv, qf, qs, q1, q2s, q3, sbuf, acc, att, c1, wvr, wr, hv, hvr, ys, yr,
    rtile, rg, ag, nat, hid, marks, chosen, wg, wu, wd, wrt, facc, mid, combine, base, turns,
    ya, yb, yc, r1a, r1b, r1c, t1a, t1b, t1c, r2a, r2b, r2c, t2a, t2b, t2c, r3a, r3b, r3c, z16,
    ld, cs, cr, q1ss, q1r, q2ss, q3r, a1s, a1r, vs, vr, vbs, vbr, ws, wrr, hs, hr, yss, yrr,
    rgs, rgr, rbs, rbr, ags, agr, abs_, abr, wds, wdr, ms, mr, rs, rr, zs, zr,
):
    n = lax.axis_index("node")
    l = lax.axis_index("local")
    core = n % 2
    at = {"z": n // 2, "y": l // 4, "x": l % 4}
    sib = (at["z"] * 2 + 1 - core, l)
    is_home = (at["x"] + at["y"]) % 2 == core
    mine = at["y"] * 2 + at["x"] // 2

    everything = pl.ds(0, 4)

    def peer(axis, p):
        if axis == "z":
            return (p * 2 + core, l)
        if axis == "y":
            return (n, p * 4 + at["x"])
        return (n, at["y"] * 4 + p)

    def slab(buf, order, q, s, val):
        idx = []
        for a in "zyx":
            if a in order[:s]:
                idx.append(everything)
            elif a == order[s]:
                idx.append(val)
            else:
                idx.append(at[a])
        return buf.at[core, q, idx[0], idx[1], idx[2]]

    def by_core(order, body):
        if isinstance(order[0], str):
            body(order)
        else:
            for c in range(2):
                pl.when(core == c)(functools.partial(body, order[c]))

    def gather_start(buf, orders, ss, rs_, q, s):
        def body(order):
            a = order[s]
            own = slab(buf, order, q, s, at[a])
            for j in range(1, 4):
                p = (at[a] + j) % 4
                send(own, own, ss.at[q, s, p], rs_.at[q, s, at[a]], peer(a, p))
        by_core(orders[q], body)

    def gather_wait(buf, orders, rs_, q, s):
        def body(order):
            a = order[s]
            for j in range(1, 4):
                p = (at[a] + j) % 4
                landed(slab(buf, order, q, s, p), rs_.at[q, s, p])
        by_core(orders[q], body)

    def gather_drain(buf, orders, ss):
        for q in range(4):
            def body(order, q=q):
                for s in range(3):
                    a = order[s]
                    for j in range(1, 4):
                        p = (at[a] + j) % 4
                        landed(slab(buf, order, q, s, at[a]), ss.at[q, s, p])
            by_core(orders[q], body)

    bar = pltpu.get_barrier_semaphore()

    def hello(device):
        pl.semaphore_signal(bar, 1, device_id=device, device_id_type=MESH)
    each(1, 16, lambda j: hello((n, (l + j) % 16)))
    each(1, 8, lambda j: hello(((n + j) % 8, l)))

    @pl.when(is_home & (mine != n))
    def _():
        each(0, 16, lambda j: hello((mine, j)))
    small = ((queries_hbm, queries), (fresh_hbm, fresh), (res_hbm, res), (owner_hbm, owner_row))
    for j, (src, dst) in enumerate(small):
        keep(src, dst, ld.at[4 + j])
    keep(cache, cv, ld.at[0])
    keep(router_hbm, router, ld.at[8])
    keep(gain_hbm, gain, ld.at[9])
    keep(w_value, wvr.at[at["z"], core], vr.at[at["z"]])
    keep(w_out.at[:, pl.ds(pl.multiple_of(n * 896, 128), 896)], wr.at[n], wrr.at[n])
    keep(w_gate, wg, ld.at[1])
    keep(w_up, wu, ld.at[2])
    own_cols = pl.ds(pl.multiple_of(core * 3584, 128), 3584)
    sib_cols = pl.ds(pl.multiple_of((1 - core) * 3584, 128), 3584)
    keep(w_down.at[:, own_cols], wd.at[0], ld.at[3])

    def deal_queries(pair):
        for k in range(8):
            lanes = pl.ds(pl.multiple_of((k * 8 + pair) * 1152, 128), 1152)
            v = queries[:, lanes].astype(F32)
            qf[pair * 2, k * 2:k * 2 + 2, :576] = v[:, :576]
            qf[pair * 2 + 1, k * 2:k * 2 + 2, :576] = v[:, 576:]
    for j, (src, dst) in enumerate(small):
        landed(dst, ld.at[4 + j])
    each(0, 8, deal_queries)
    qs[:, :, :576] = qf[:, :, :576].astype(BF)
    qs[:, :, 576:] = jnp.zeros((16, 16, 64), BF)
    own_band = iota((16, 576), 1) // 64 == iota((16, 576), 0)
    fold = (iota((576, 64), 0) % 64 == iota((576, 64), 1)).astype(BF)
    new = fresh[...].astype(F32)
    for t in range(2):
        bands = jnp.where(own_band, jnp.broadcast_to(new[t:t + 1], (16, 576)), 0.0).astype(BF)
        qs[t, :, 576:640] = jnp.dot(bands, fold, preferred_element_type=F32).astype(BF)

    r = res[...].astype(F32)
    line = iota((16, 896), 0)
    tile = jnp.zeros((16, 896), F32)
    mark = jnp.zeros((16, 128), F32)
    for t in range(2):
        for k in range(8):
            tile = jnp.where(line == t * 8 + k, jnp.broadcast_to(r[t:t + 1, k * 896:(k + 1) * 896], (16, 896)), tile)
        hit = iota((16, 128), 1) == ids[t, 0]
        for j in range(1, 8):
            hit = hit | (iota((16, 128), 1) == ids[t, j])
        mark = jnp.where(hit & (iota((16, 128), 0) == t * 8), 1.0, mark)
    rtile[...] = jnp.concatenate([tile, mark], axis=1).astype(BF)
    for q in range(4):
        rg[core, q, at["z"], at["y"], at["x"]] = rtile[:, q * 256:(q + 1) * 256]

    landed(cv, ld.at[0])

    def cache_pick(t):
        pick = jnp.int32(0)
        for i in range(8):
            pick = jnp.where(owner[n * 8 + i] // 16 == t, i, pick)
        csend[t] = cv[pick]
    each(0, 8, cache_pick)
    pl.semaphore_wait(bar, 29)

    keep(qs.at[l], q1.at[l], q1r.at[l])

    def q_first(j):
        p = (l + j) % 16
        send(qs.at[p], q1.at[l], q1ss.at[p], q1r.at[l], (n, p))
    each(1, 16, q_first)
    if RG0_EARLY:
        for q in range(4):
            gather_start(rg, RESIDUAL, rgs, rgr, q, 0)

    def cache_send(i):
        dx = jnp.where(is_home, EVEN[i][0], ODD[i][0])
        dy = jnp.where(is_home, EVEN[i][1], ODD[i][1])
        px, py = (at["x"] + dx) % 4, (at["y"] + dy) % 4
        t, dest = py * 2 + px // 2, py * 4 + px

        @pl.when(dest == l)
        def _():
            keep(csend.at[t], crecv.at[l], cr.at[l])

        @pl.when(dest != l)
        def _():
            send(csend.at[t], crecv.at[l], cs.at[t], cr.at[l], (n, dest))
    for i in range(CACHE_FIRST):
        cache_send(i)

    def v_send():
        for j in range(1, 4):
            p = (at["z"] + j) % 4
            send(w_value, wvr.at[at["z"], core], vs.at[p], vr.at[at["z"]], peer("z", p))
    if V_EARLY:
        v_send()

    each(0, 16, lambda j: landed(q1.at[j], q1r.at[j]))

    def q_second(j):
        p = (n + j) % 8
        pick = jnp.int32(0)
        for i in range(8):
            o = owner[p * 8 + i]
            pick = jnp.where(o // 16 == n, o % 16, pick)
        q2s[p] = q1[pick]
        dest = home_local(p, n)
        self_ = (p == n) & (dest == l)

        @pl.when(self_)
        def _():
            keep(q2s.at[p], q3.at[l], q3r.at[l])

        @pl.when(jnp.logical_not(self_))
        def _():
            send(q2s.at[p], q3.at[l], q2ss.at[p], q3r.at[l], (p, dest))
    each(0, 8, q_second)
    for i in range(CACHE_FIRST, 8):
        cache_send(i)

    if not V_EARLY:
        v_send()
    if not RG0_EARLY:
        for q in range(4):
            gather_start(rg, RESIDUAL, rgs, rgr, q, 0)

    def w_send(j):
        p = (n + j) % 8
        send(w_out.at[:, pl.ds(pl.multiple_of(p * 896, 128), 896)], wr.at[n], ws.at[p], wrr.at[n], (p, l))
    each(1, 8, w_send)
    send(w_down.at[:, sib_cols], wd.at[1], wds, wdr, sib)
    def rg1():
        for q in range(4):
            gather_wait(rg, RESIDUAL, rgr, q, 0)
            gather_start(rg, RESIDUAL, rgs, rgr, q, 1)

    def rg2(phase):
        for q in range(4):
            if RG2_AT[q] == phase:
                gather_wait(rg, RESIDUAL, rgr, q, 1)
                gather_start(rg, RESIDUAL, rgs, rgr, q, 2)
    if RG1_AT == 0:
        rg1()

    landed(router, ld.at[8])
    landed(gain, ld.at[9])
    wt = router[...]
    hi = wt.astype(BF)
    rest = wt - hi.astype(F32)
    mi = rest.astype(BF)
    wrt[0:16, :] = hi
    wrt[16:32, :] = mi
    wrt[32:48, :] = (rest - mi.astype(F32)).astype(BF)
    wrt[48:128, :] = jnp.zeros((80, 7168), BF)

    i64 = iota((256, 64), 0)
    spot = row_of(owner_row[...], i64 // 2, i64 % 2)
    to_nat = jnp.where(iota((256, 256), 1) == spot, 1.0, 0.0)
    turns[3] = to_nat.T.astype(BF)
    for k, (lo, width, order) in enumerate(PARTS):
        digit = {order[0]: i64 // 64, order[1]: i64 // 16 % 4, order[2]: i64 // 4 % 4}
        s64 = (digit["z"] * 2 + i64 // 2 % 2) * 16 + digit["y"] * 4 + digit["x"]
        turns[k] = (iota((256, 256), 1) == row_of(owner_row[...], s64, i64 % 2)).astype(BF)

    for j in range(4):
        landed(wvr.at[j, core], vr.at[j])
    send(wvr.at[:, core], wvr.at[:, core], vbs, vbr, sib)

    def cache_left(t):
        @pl.when(home_local(n, t) != l)
        def _():
            landed(csend.at[t], cs.at[t])
    each(0, 8, cache_left)

    @pl.when(is_home)
    def _():
        each(0, 16, lambda j: landed(crecv.at[j], cr.at[j]))
    if RG1_AT == 1:
        rg1()
    rg2(0)

    @pl.when(is_home)
    def _():
        each(0, 16, lambda j: landed(q3.at[j], q3r.at[j]))
        length = jnp.int32(0)
        for i in range(8):
            r = n * 8 + i
            length = jnp.where(owner[r] // 16 == mine, lengths[r], length)
        q = q3[...].reshape(256, 640)[:, :576]
        spread = (iota((64, 576), 1) % 64 == iota((64, 576), 0)).astype(BF)
        rows = []
        for t in range(2):
            wide = jnp.dot(q3[t][:, 576:640], spread, preferred_element_type=F32)
            rows.append(jnp.sum(jnp.where(own_band, wide, 0.0), axis=0, keepdims=True))
        up = iota((128, 576), 0)
        fresh_rows = jnp.where(up == 0, rows[0], jnp.where(up == 1, rows[1], 0.0)).astype(BF)
        fs = lax.dot_general(q, fresh_rows, NT, preferred_element_type=F32) * score_scale
        fs = jnp.where(iota((256, 128), 1) <= iota((256, 128), 0) % 2, fs, -jnp.inf)

        def score(p, top):
            keys = jnp.concatenate([crecv[2 * p], crecv[2 * p + 1]], axis=1)
            s = jnp.dot(q, keys, preferred_element_type=F32) * score_scale
            s = jnp.where(p * 256 + iota((256, 256), 1) < length, s, -jnp.inf)
            sbuf[p] = s
            return jnp.maximum(top, jnp.max(s, axis=1, keepdims=True))
        top = lax.fori_loop(0, 8, score, jnp.max(fs, axis=1, keepdims=True))
        fe = jnp.exp(fs - top)
        acc[...] = jnp.dot(fe.astype(BF), fresh_rows[:, :512], preferred_element_type=F32)

        def weigh(p, total):
            e = jnp.exp(sbuf[p] - top)
            values = jnp.concatenate([crecv[2 * p, :512, :], crecv[2 * p + 1, :512, :]], axis=1)
            acc[...] += lax.dot_general(e.astype(BF), values, NT, preferred_element_type=F32)
            return total + jnp.sum(e, axis=1, keepdims=True)
        total = lax.fori_loop(0, 8, weigh, jnp.sum(fe, axis=1, keepdims=True))
        att[...] = (acc[...] / total).astype(BF).reshape(16, 16, 512)

        keep(att.at[l], c1.at[mine], a1r.at[mine])

        def head_local(j):
            p = (l + j) % 16
            send(att.at[p], c1.at[mine], a1s.at[p], a1r.at[mine], (n, p))
        each(1, 16, head_local)

    if RG1_AT == 2:
        rg1()
    rg2(1)

    landed(wvr.at[:, 1 - core], vbr)
    each(0, 8, lambda j: landed(c1.at[j], a1r.at[j]))
    to = iota((128, 128), 0)
    perm = (iota((128, 128), 1) == (to // 2 % 8) * 16 + (to // 16) * 2 + to % 2).astype(BF)
    by_head = jnp.dot(perm, c1[...].reshape(128, 512), preferred_element_type=F32).astype(BF)
    for k in range(8):
        hv[:, k * 128:(k + 1) * 128] = jnp.dot(
            by_head[k * 16:(k + 1) * 16], wvr[k // 2, k % 2], preferred_element_type=F32
        ).astype(BF)
    keep(hv, hvr.at[n], hr.at[n])

    def values_out(j):
        p = (n + j) % 8
        send(hv, hvr.at[n], hs.at[p], hr.at[n], (p, l))
    each(1, 8, values_out)
    rg2(2)

    def rg_sib(last):
        for q in range(4):
            if (RG2_AT[q] <= 1) != last:
                gather_wait(rg, RESIDUAL, rgr, q, 2)
                send(rg.at[core, q], rg.at[core, q], rbs.at[q], rbr.at[q], sib)
    rg_sib(False)
    each(0, 8, lambda j: landed(wr.at[j], wrr.at[j]))
    each(0, 8, lambda j: landed(hvr.at[j], hr.at[j]))
    proj = jnp.dot(
        hvr[...].reshape(128, 1024), wr[...].reshape(1024, 896), preferred_element_type=F32
    ).reshape(16, 8, 896)
    high = jnp.concatenate([proj[:, :, 512:], jnp.zeros((16, 8, 128), F32)], axis=2)
    ys[...] = jnp.concatenate([proj[:, :, :512], high], axis=1).astype(BF)
    keep(ys.at[l], yr.at[l], yrr.at[l])

    def rows_out(j):
        p = (l + j) % 16
        send(ys.at[p], yr.at[l], yss.at[p], yrr.at[l], (n, p))
    each(1, 16, rows_out)
    rg2(3)

    deal = (iota((128, 128), 1) == (to % 16) * 8 + to // 16).astype(BF)

    def unpack(g):
        rows = pl.ds(pl.multiple_of(g * 16, 16), 16)
        z, c, y2 = g // 4, g // 2 % 2, g % 2
        x = jnp.concatenate(
            [rg[c, q, z, pl.ds(y2 * 2, 2)].reshape(128, 256) for q in range(4)], axis=1
        )
        d = jnp.dot(deal, x, preferred_element_type=F32).astype(BF)
        for k in range(8):
            nat[rows, k * 896:(k + 1) * 896] = d[k * 16:(k + 1) * 16, :896]
        marks[rows, :] = d[:16, 896:]

    def reorder(k):
        cols = pl.ds(pl.multiple_of(k * 896, 128), 896)
        hid[:, cols] = jnp.dot(turns[3], nat[:, cols], preferred_element_type=F32).astype(BF)

    def products(half, k, wide):
        cols = pl.ds(pl.multiple_of(k * 896, 128), 896)
        hg = (wide * gain[:, cols]).astype(BF)
        rows = pl.ds(half * 128, 128)
        facc[rows, :256] += jnp.dot(hg, wg[cols, :], preferred_element_type=F32)
        facc[rows, 256:512] += jnp.dot(hg, wu[cols, :], preferred_element_type=F32)
        facc[rows, 512:] += lax.dot_general(hg, wrt[:, cols], NT, preferred_element_type=F32)
        return jnp.sum(wide * wide, axis=1, keepdims=True)

    def activate(half, squares):
        rows = pl.ds(half * 128, 128)
        factor = lax.rsqrt(squares * (1.0 / 7168) + norm_eps)
        gated = facc[rows, :256] * factor
        lifted = facc[rows, 256:512] * factor
        mid[0, half] = (gated * jax.nn.sigmoid(gated) * lifted).astype(BF)
        send(mid.at[0, half], mid.at[1, half], ms.at[half], mr.at[half], sib)
        three = facc[rows, 512:]
        logits = three + pltpu.roll(three, 112, 1) + pltpu.roll(three, 96, 1)
        affinity = jax.nn.sigmoid(logits * factor)
        picked = jnp.where(chosen[rows, :] > 0.5, affinity, 0.0)
        share = picked / jnp.sum(picked, axis=1, keepdims=True) * route_scale
        combine[rows, :] = share.astype(BF)

    def resting(k, squares):
        cols = pl.ds(pl.multiple_of(k * 896, 128), 896)
        return squares + products(1, k, hid[128:, cols].astype(F32))

    facc[...] = jnp.zeros_like(facc)
    if UNPACK_FIRST:
        rg_sib(True)
        for q in range(4):
            landed(rg.at[1 - core, q], rbr.at[q])
    each(0, UNPACK_FIRST, unpack)
    each(0, 16, lambda j: landed(yr.at[j], yrr.at[j]))
    tot = yr[0].astype(F32)
    for j in range(1, 16):
        tot = tot + yr[j].astype(F32)
    shard = tot.astype(BF)
    for q in range(4):
        ag[core, q, at["z"], at["y"], at["x"]] = shard[:, q * 128:(q + 1) * 128]
        gather_start(ag, GATHER, ags, agr, q, 0)
    if not UNPACK_FIRST:
        rg_sib(True)
        for q in range(4):
            landed(rg.at[1 - core, q], rbr.at[q])
    each(UNPACK_FIRST, 16, unpack)
    for q in range(4):
        gather_wait(ag, GATHER, agr, q, 0)
        gather_start(ag, GATHER, ags, agr, q, 1)
    each(0, 8, reorder)
    for q in range(4):
        gather_wait(ag, GATHER, agr, q, 1)
        gather_start(ag, GATHER, ags, agr, q, 2)
    chosen[...] = jnp.dot(turns[3], marks[...], preferred_element_type=F32)
    landed(wg, ld.at[1])
    landed(wu, ld.at[2])
    activate(1, lax.fori_loop(0, 8, resting, jnp.zeros((128, 1), F32)))
    for q in range(4):
        gather_wait(ag, GATHER, agr, q, 2)
        send(ag.at[core, q], ag.at[core, q], abs_.at[q], abr.at[q], sib)

    def serving(c):
        def step(z, squares):
            tops, lows = [], []
            for q in range(4):
                b = ag[c, q, z].reshape(16, 16, 128).astype(F32)
                tops.append(b[:, :8].reshape(128, 128))
                lows.append(b[:, 8:].reshape(128, 128))
            attn = jnp.concatenate(tops + lows[:3], axis=1)
            k = z * 2 + c
            cols = pl.ds(pl.multiple_of(k * 896, 128), 896)
            h = (hid[:128, cols].astype(F32) + attn).astype(BF)
            hid[:128, cols] = h
            return squares + products(0, k, h.astype(F32))
        return step
    squares = lax.fori_loop(0, 4, serving(core), jnp.zeros((128, 1), F32))
    for q in range(4):
        landed(ag.at[1 - core, q], abr.at[q])
    activate(0, lax.fori_loop(0, 4, serving(1 - core), squares))

    lane = iota((256, 128), 1)
    e_own, e_sib = n * 2 + l // 8, sib[0] * 2 + l // 8
    landed(wd.at[0], ld.at[3])
    landed(wd.at[1], wdr)
    for half in range(2):
        landed(mid.at[1, half], mr.at[half])

    ybuf, r1, t1 = (ya, yb, yc), (r1a, r1b, r1c), (t1a, t1b, t1c)
    r2, t2, r3 = (r2a, r2b, r2c), (t2a, t2b, t2c), (r3a, r3b, r3c)
    for k, (lo, width, order) in enumerate(PARTS):
        m0 = jnp.dot(turns[k], mid[0].reshape(256, 256), preferred_element_type=F32).astype(BF)
        m1 = jnp.dot(turns[k], mid[1].reshape(256, 256), preferred_element_type=F32).astype(BF)
        cw = jnp.dot(turns[k], combine[...], preferred_element_type=F32)
        w0 = jnp.sum(jnp.where(lane == e_own, cw, 0.0), axis=1, keepdims=True)
        w1 = jnp.sum(jnp.where(lane == e_sib, cw, 0.0), axis=1, keepdims=True)
        cn = 384 if width % 384 == 0 else 640
        for c0 in range(0, width, cn):
            a = jnp.dot(m0, wd[0, :, lo + c0:lo + c0 + cn], preferred_element_type=F32) * w0
            b = jnp.dot(m1, wd[1, :, lo + c0:lo + c0 + cn], preferred_element_type=F32) * w1
            ybuf[k][:, :, c0:c0 + cn] = (a + b).astype(BF).reshape(4, 64, cn)
        a1 = order[0]
        for j in range(1, 4):
            p = (at[a1] + j) % 4
            send(ybuf[k].at[p], r1[k].at[at[a1]], rs.at[k, 0, p], rr.at[k, 0, at[a1]], peer(a1, p))

    s16 = iota((16, 64), 0) * 0 + (n * 16 + l)
    own_rows = row_of(owner_row[...], s16, iota((16, 64), 0) % 2)
    sel = (iota((16, 256), 1) == own_rows).astype(BF)
    for k in range(4):
        base[:, k * 1792:(k + 1) * 1792] = jnp.dot(
            sel, hid[:, k * 1792:(k + 1) * 1792], preferred_element_type=F32
        )

    for k, (lo, width, order) in enumerate(PARTS):
        a1, a2 = order[0], order[1]
        tot = ybuf[k][at[a1]].astype(F32)
        for j in range(1, 4):
            p = (at[a1] + j) % 4
            landed(r1[k].at[p], rr.at[k, 0, p])
            tot = tot + r1[k][p].astype(F32)
        t1[k][...] = tot.astype(BF).reshape(4, 16, width)
        for j in range(1, 4):
            p = (at[a2] + j) % 4
            send(t1[k].at[p], r2[k].at[at[a2]], rs.at[k, 1, p], rr.at[k, 1, at[a2]], peer(a2, p))
    for k, (lo, width, order) in enumerate(PARTS):
        a2, a3 = order[1], order[2]
        tot = t1[k][at[a2]].astype(F32)
        for j in range(1, 4):
            p = (at[a2] + j) % 4
            landed(r2[k].at[p], rr.at[k, 1, p])
            tot = tot + r2[k][p].astype(F32)
        t2[k][...] = tot.astype(BF)
        for j in range(1, 4):
            p = (at[a3] + j) % 4
            send(t2[k], r3[k].at[at[a3]], rs.at[k, 2, p], rr.at[k, 2, at[a3]], peer(a3, p))
    for k, (lo, width, order) in enumerate(PARTS):
        a3 = order[2]
        tot = t2[k][...].astype(F32)
        for j in range(1, 4):
            p = (at[a3] + j) % 4
            landed(r3[k].at[p], rr.at[k, 2, p])
            tot = tot + r3[k][p].astype(F32)
        z16[core, :, lo:lo + width] = tot.astype(BF)
    send(z16.at[core], z16.at[core], zs, zr, sib)
    landed(z16.at[1 - core], zr)

    up, dn = iota((16, 16), 0), iota((16, 16), 1)
    for half in range(2):
        for k, (lo, width, order) in enumerate(PARTS):
            c0 = half * 3584 + lo
            pickz = ((up < 2) & (dn == at[order[2]] * 4 + core * 2 + up)).astype(BF)
            mix = jnp.dot(pickz, z16[half, :, lo:lo + width], preferred_element_type=F32)
            out[:, c0:c0 + width] = (base[:, c0:c0 + width] + mix)[:2].astype(BF)

    def drain(j):
        p = (l + j) % 16
        landed(qs.at[p], q1ss.at[p])
        landed(ys.at[p], yss.at[p])

        @pl.when(is_home)
        def _():
            landed(att.at[p], a1s.at[p])
    each(1, 16, drain)

    def drain_home(t):
        @pl.when(jnp.logical_not((t == n) & (home_local(t, n) == l)))
        def _():
            landed(q2s.at[t], q2ss.at[t])
    each(0, 8, drain_home)

    def drain_node(j):
        p = (n + j) % 8
        landed(hv, hs.at[p])
        landed(wr.at[p], ws.at[p])
    each(1, 8, drain_node)
    for j in range(1, 4):
        p = (at["z"] + j) % 4
        landed(wvr.at[p, core], vs.at[p])
    landed(wvr.at[:, core], vbs)
    gather_drain(rg, RESIDUAL, rgs)
    gather_drain(ag, GATHER, ags)
    for q in range(4):
        landed(rg.at[core, q], rbs.at[q])
        landed(ag.at[core, q], abs_.at[q])
    landed(wd.at[1], wds)
    for half in range(2):
        landed(mid.at[0, half], ms.at[half])
    landed(z16.at[core], zs)
    for k, (lo, width, order) in enumerate(PARTS):
        for s, buf in enumerate((ybuf[k], t1[k], t2[k])):
            for j in range(1, 4):
                p = (at[order[s]] + j) % 4
                landed(buf if s == 2 else buf.at[p], rs.at[k, s, p])


def layer(owner, lengths, ids, queries, fresh, res, gain, router, cache, w_value, w_out, w_gate, w_up, w_down):
    dma = pltpu.SemaphoreType.DMA
    vm = pl.BlockSpec(memory_space=pltpu.VMEM)
    sm = pl.BlockSpec(memory_space=pltpu.SMEM)
    hbm = pl.BlockSpec(memory_space=pl.ANY)
    bf = lambda *shape: pltpu.VMEM(shape, BF)
    f32 = lambda *shape: pltpu.VMEM(shape, F32)
    return pl.pallas_call(
        kernel,
        name="layer",
        out_shape=jax.ShapeDtypeStruct((2, 7168), BF),
        in_specs=[sm, sm, sm] + [hbm] * 12,
        out_specs=vm,
        scratch_shapes=[
            pltpu.VMEM((1, 64), jnp.int32), bf(2, 73728), bf(2, 576), bf(2, 7168), f32(1, 7168), f32(16, 7168),
            bf(8, 576, 128), bf(8, 576, 128), bf(16, 576, 128),
            f32(16, 16, 640), bf(16, 16, 640), bf(16, 16, 640), bf(8, 16, 640), bf(16, 16, 640),
            f32(8, 256, 256), f32(256, 512), bf(16, 16, 512), bf(8, 16, 512),
            bf(4, 2, 512, 128), bf(8, 128, 896), bf(16, 1024), bf(8, 16, 1024),
            bf(16, 16, 512), bf(16, 16, 512),
            bf(16, 1024), bf(2, 4, 4, 4, 4, 16, 256), bf(2, 4, 4, 4, 4, 16, 128),
            bf(256, 7168), bf(256, 7168), bf(256, 128), f32(256, 128),
            bf(7168, 256), bf(7168, 256), bf(2, 256, 3584), bf(128, 7168),
            f32(256, 640), bf(2, 2, 128, 256), bf(256, 128), f32(16, 7168), bf(4, 256, 256),
        ]
        + [bf(4, 64, w) for w in WIDTHS] + [bf(4, 64, w) for w in WIDTHS]
        + [bf(4, 16, w) for w in WIDTHS] + [bf(4, 16, w) for w in WIDTHS]
        + [bf(16, w) for w in WIDTHS] + [bf(4, 16, w) for w in WIDTHS]
        + [bf(2, 16, 3584)]
        + [dma((k,)) for k in (10, 8, 16, 16, 16, 8, 16, 16, 8, 4, 4)]
        + [dma, dma]
        + [dma((k,)) for k in (8, 8, 8, 8, 16, 16)]
        + [
            dma((4, 3, 4)), dma((4, 3, 4)), dma((4,)), dma((4,)),
            dma((4, 3, 4)), dma((4, 3, 4)), dma((4,)), dma((4,)),
            dma, dma, dma((2,)), dma((2,)), dma((3, 3, 4)), dma((3, 3, 4)), dma, dma,
        ],
        compiler_params=pltpu.CompilerParams(
            collective_id=0, has_side_effects=True, vmem_limit_bytes=58 << 20
        ),
    )(owner, lengths, ids, owner[None, :], queries, fresh, res, gain, router, cache, w_value, w_out, w_gate, w_up, w_down)


def shards(
    latent_cache, lengths, owner_map, queries, new_latent, residual, w_value, w_out,
    norm_gain, w_router, expert_ids, w_gate, w_up, w_down,
):
    out = layer(
        owner_map, lengths, expert_ids[0], queries[0], new_latent[0], residual[0], norm_gain[None, :], w_router.T,
        latent_cache, w_value[0], w_out, w_gate, w_up, w_down,
    )
    return out[None]


def solution(mesh):
    both = ("node", "local")
    in_specs = (
        P("node", None, "local"), P(), P(), P(both, None, None), P(both, None, None),
        P(both, None, None), P(both, None, None), P(both, None), P(), P(),
        P(both, None, None), P(None, both), P(None, both), P(both, None),
    )
    return jax.shard_map(
        shards, mesh=mesh, in_specs=in_specs, out_specs=P(both, None, None), check_vma=False
    )
```

time: 127 us -> 108 us (0.85)
  Pallas kernels: 123 us -> 106 us
  local copies, waits for them, and re-layouts: 3.95 us -> 1.38 us
    pallas_call x1, Pallas kernels: 123 us -> 106 us  [layer(): pl.pallas_call(kernel, name='layer', out_shape=jax.ShapeDtypeStruct((2, 7...]
    reshape x3 -> x0, local copies, waits for them, and re-layouts: 2.57 us -> none  [shards(): queries.reshape(2, 8, 16, 576).transpose(2, 1, 0, 3).reshape(16, 16, 576)]
where the time goes in v3:
time: 108 us; the launch traced here: 107 us
  Pallas kernels  106 us (98%)
  local copies, waits for them, and re-layouts  1.38 us (1%)
    pallas_call x1, Pallas kernels, layer(): pl.pallas_call(kernel, name='layer', out_shape=jax.ShapeDtypeStruct((2, 7...  106 us

profile of v3, /device:TPU:1, one launch (start us, length us, event | category | flops | bytes accessed | tf_op | source)
XLA Modules:
  0.0 107.5 jit_solution(6099928924826854442)
XLA Ops:
  0.0 106.1 %layer.1 = bf16[2,7168]{1,0:T(2,128)(2,1)} custom-call(s32[64]{0:T(128)} %owner.1, s32[64]{0:T(128)} %lengths.1, s32[2,8]{1,0:T(2,128)} %bitcast.17, s32[1,64]{1,0:T(1,128)} %bitcast.16, bf16[2,73728]{1,0:T(2,128)(2,1)} %bitcast.10, bf16[2,576]{1,0:T(2,128)(2,1)} %bitcast.15, bf16[2,7168]{1,0:T(2,128)(2,1)} %bitcast.13, f32[1,7168]{1,0:T(1,128)} %bitcast.14, ...), custom_call_target="tpu_custom_call" | custom-call | tf_op jit(solution)/shard_map/layer/pallas_call | solution.py:630
  106.1 1.4 %copy.16 = bf16[1,2,7168]{2,1,0:T(2,128)(2,1)} copy(bf16[1,2,7168]{2,1,0:T(2,128)(2,1)} %bitcast.12) | data formatting | bytes 57344

commit v4 on v3

--- a/solution.py
+++ b/solution.py
@@ -49,7 +49,7 @@
 
 GATHER = (("y", "z", "x"), ("z", "x", "y"), ("x", "y", "z"), (("y", "z", "x"), ("z", "x", "y")))
 RESIDUAL = (("z", "y", "x"), ("z", "x", "y"), ("z", "y", "x"), ("z", "x", "y"))
-CACHE_FIRST = 4
+CACHE_FIRST = 5
 RG0_EARLY = 1
 V_EARLY = 1
 RG1_AT = 1
@@ -57,6 +57,11 @@
 EVEN = ((1, 1), (3, 3), (1, 3), (3, 1), (2, 0), (0, 2), (2, 2), (0, 0))
 ODD = ((1, 0), (3, 0), (0, 1), (0, 3), (1, 2), (3, 2), (2, 1), (2, 3))
 UNPACK_FIRST = 12
+RG_LATE = 0
+THROTTLE = 1
+WD_LATE = 1
+SIB_AT = 0
+W_LATE = 0
 PARTS = ((0, 1280, ("x", "y", "z")), (1280, 1152, ("y", "z", "x")), (2432, 1152, ("z", "x", "y")))
 WIDTHS = tuple(w for _, w, _ in PARTS)
 
@@ -94,7 +99,7 @@
             return (n, p * 4 + at["x"])
         return (n, at["y"] * 4 + p)
 
-    def slab(buf, order, q, s, val):
+    def slab(buf, order, q, s, val, c=None):
         idx = []
         for a in "zyx":
             if a in order[:s]:
@@ -103,7 +108,7 @@
                 idx.append(val)
             else:
                 idx.append(at[a])
-        return buf.at[core, q, idx[0], idx[1], idx[2]]
+        return buf.at[core if c is None else c, q, idx[0], idx[1], idx[2]]
 
     def by_core(order, body):
         if isinstance(order[0], str):
@@ -146,15 +151,16 @@
     each(1, 16, lambda j: hello((n, (l + j) % 16)))
     each(1, 8, lambda j: hello(((n + j) % 8, l)))
 
-    @pl.when(is_home & (mine != n))
-    def _():
-        each(0, 16, lambda j: hello((mine, j)))
     small = ((queries_hbm, queries), (fresh_hbm, fresh), (res_hbm, res), (owner_hbm, owner_row))
     for j, (src, dst) in enumerate(small):
         keep(src, dst, ld.at[4 + j])
     keep(cache, cv, ld.at[0])
     keep(router_hbm, router, ld.at[8])
     keep(gain_hbm, gain, ld.at[9])
+
+    @pl.when(is_home & (mine != n))
+    def _():
+        each(0, 16, lambda j: hello((mine, j)))
     keep(w_value, wvr.at[at["z"], core], vr.at[at["z"]])
     keep(w_out.at[:, pl.ds(pl.multiple_of(n * 896, 128), 896)], wr.at[n], wrr.at[n])
     keep(w_gate, wg, ld.at[1])
@@ -181,6 +187,46 @@
         bands = jnp.where(own_band, jnp.broadcast_to(new[t:t + 1], (16, 576)), 0.0).astype(BF)
         qs[t, :, 576:640] = jnp.dot(bands, fold, preferred_element_type=F32).astype(BF)
 
+    pl.semaphore_wait(bar, 29)
+
+    keep(qs.at[l], q1.at[l], q1r.at[l])
+
+    def q_first(j):
+        p = (l + j) % 16
+        send(qs.at[p], q1.at[l], q1ss.at[p], q1r.at[l], (n, p))
+    each(1, 16, q_first)
+    landed(cv, ld.at[0])
+
+    def cache_pick(t):
+        pick = jnp.int32(0)
+        for i in range(8):
+            pick = jnp.where(owner[n * 8 + i] // 16 == t, i, pick)
+        csend[t] = cv[pick]
+    each(0, 8, cache_pick)
+
+    def cache_send(i):
+        dx = jnp.where(is_home, EVEN[i][0], ODD[i][0])
+        dy = jnp.where(is_home, EVEN[i][1], ODD[i][1])
+        px, py = (at["x"] + dx) % 4, (at["y"] + dy) % 4
+        t, dest = py * 2 + px // 2, py * 4 + px
+
+        @pl.when(dest == l)
+        def _():
+            keep(csend.at[t], crecv.at[l], cr.at[l])
+
+        @pl.when(dest != l)
+        def _():
+            send(csend.at[t], crecv.at[l], cs.at[t], cr.at[l], (n, dest))
+    for i in range(CACHE_FIRST):
+        cache_send(i)
+
+    def v_send():
+        for j in range(1, 4):
+            p = (at["z"] + j) % 4
+            send(w_value, wvr.at[at["z"], core], vs.at[p], vr.at[at["z"]], peer("z", p))
+    if V_EARLY:
+        v_send()
+
     r = res[...].astype(F32)
     line = iota((16, 896), 0)
     tile = jnp.zeros((16, 896), F32)
@@ -195,49 +241,9 @@
     rtile[...] = jnp.concatenate([tile, mark], axis=1).astype(BF)
     for q in range(4):
         rg[core, q, at["z"], at["y"], at["x"]] = rtile[:, q * 256:(q + 1) * 256]
-
-    landed(cv, ld.at[0])
-
-    def cache_pick(t):
-        pick = jnp.int32(0)
-        for i in range(8):
-            pick = jnp.where(owner[n * 8 + i] // 16 == t, i, pick)
-        csend[t] = cv[pick]
-    each(0, 8, cache_pick)
-    pl.semaphore_wait(bar, 29)
-
-    keep(qs.at[l], q1.at[l], q1r.at[l])
-
-    def q_first(j):
-        p = (l + j) % 16
-        send(qs.at[p], q1.at[l], q1ss.at[p], q1r.at[l], (n, p))
-    each(1, 16, q_first)
     if RG0_EARLY:
         for q in range(4):
             gather_start(rg, RESIDUAL, rgs, rgr, q, 0)
-
-    def cache_send(i):
-        dx = jnp.where(is_home, EVEN[i][0], ODD[i][0])
-        dy = jnp.where(is_home, EVEN[i][1], ODD[i][1])
-        px, py = (at["x"] + dx) % 4, (at["y"] + dy) % 4
-        t, dest = py * 2 + px // 2, py * 4 + px
-
-        @pl.when(dest == l)
-        def _():
-            keep(csend.at[t], crecv.at[l], cr.at[l])
-
-        @pl.when(dest != l)
-        def _():
-            send(csend.at[t], crecv.at[l], cs.at[t], cr.at[l], (n, dest))
-    for i in range(CACHE_FIRST):
-        cache_send(i)
-
-    def v_send():
-        for j in range(1, 4):
-            p = (at["z"] + j) % 4
-            send(w_value, wvr.at[at["z"], core], vs.at[p], vr.at[at["z"]], peer("z", p))
-    if V_EARLY:
-        v_send()
 
     each(0, 16, lambda j: landed(q1.at[j], q1r.at[j]))
 
@@ -271,8 +277,13 @@
     def w_send(j):
         p = (n + j) % 8
         send(w_out.at[:, pl.ds(pl.multiple_of(p * 896, 128), 896)], wr.at[n], ws.at[p], wrr.at[n], (p, l))
-    each(1, 8, w_send)
-    send(w_down.at[:, sib_cols], wd.at[1], wds, wdr, sib)
+    if not W_LATE:
+        each(1, 8, w_send)
+
+    def wd_send():
+        send(w_down.at[:, sib_cols], wd.at[1], wds, wdr, sib)
+    if not WD_LATE:
+        wd_send()
     def rg1():
         for q in range(4):
             gather_wait(rg, RESIDUAL, rgr, q, 0)
@@ -306,6 +317,9 @@
         s64 = (digit["z"] * 2 + i64 // 2 % 2) * 16 + digit["y"] * 4 + digit["x"]
         turns[k] = (iota((256, 256), 1) == row_of(owner_row[...], s64, i64 % 2)).astype(BF)
 
+    if W_LATE:
+        each(1, 8, w_send)
+
     for j in range(4):
         landed(wvr.at[j, core], vr.at[j])
     send(wvr.at[:, core], wvr.at[:, core], vbs, vbr, sib)
@@ -314,11 +328,8 @@
         @pl.when(home_local(n, t) != l)
         def _():
             landed(csend.at[t], cs.at[t])
-    each(0, 8, cache_left)
-
-    @pl.when(is_home)
-    def _():
-        each(0, 16, lambda j: landed(crecv.at[j], cr.at[j]))
+    if THROTTLE == 1:
+        each(0, 8, cache_left)
     if RG1_AT == 1:
         rg1()
     rg2(0)
@@ -341,10 +352,22 @@
         fs = lax.dot_general(q, fresh_rows, NT, preferred_element_type=F32) * score_scale
         fs = jnp.where(iota((256, 128), 1) <= iota((256, 128), 0) % 2, fs, -jnp.inf)
 
+        def source(i, table):
+            dx, dy = jnp.int32(table[0][0]), jnp.int32(table[0][1])
+            for j in range(1, 8):
+                dx = jnp.where(i == j, table[j][0], dx)
+                dy = jnp.where(i == j, table[j][1], dy)
+            return (at["y"] - dy + 4) % 4 * 4 + (at["x"] - dx + 4) % 4
+
         def score(p, top):
-            keys = jnp.concatenate([crecv[2 * p], crecv[2 * p + 1]], axis=1)
+            le, lo = source(p, EVEN), source(p, ODD)
+            landed(crecv.at[le], cr.at[le])
+            landed(crecv.at[lo], cr.at[lo])
+            keys = jnp.concatenate([crecv[le], crecv[lo]], axis=1)
             s = jnp.dot(q, keys, preferred_element_type=F32) * score_scale
-            s = jnp.where(p * 256 + iota((256, 256), 1) < length, s, -jnp.inf)
+            lane = iota((256, 256), 1)
+            place = lane + jnp.where(lane < 128, le * 128, lo * 128 - 128)
+            s = jnp.where(place < length, s, -jnp.inf)
             sbuf[p] = s
             return jnp.maximum(top, jnp.max(s, axis=1, keepdims=True))
         top = lax.fori_loop(0, 8, score, jnp.max(fs, axis=1, keepdims=True))
@@ -353,7 +376,8 @@
 
         def weigh(p, total):
             e = jnp.exp(sbuf[p] - top)
-            values = jnp.concatenate([crecv[2 * p, :512, :], crecv[2 * p + 1, :512, :]], axis=1)
+            le, lo = source(p, EVEN), source(p, ODD)
+            values = jnp.concatenate([crecv[le, :512, :], crecv[lo, :512, :]], axis=1)
             acc[...] += lax.dot_general(e.astype(BF), values, NT, preferred_element_type=F32)
             return total + jnp.sum(e, axis=1, keepdims=True)
         total = lax.fori_loop(0, 8, weigh, jnp.sum(fe, axis=1, keepdims=True))
@@ -368,10 +392,13 @@
 
     if RG1_AT == 2:
         rg1()
+    if WD_LATE:
+        wd_send()
     rg2(1)
 
     landed(wvr.at[:, 1 - core], vbr)
     each(0, 8, lambda j: landed(c1.at[j], a1r.at[j]))
+    rg2(5)
     to = iota((128, 128), 0)
     perm = (iota((128, 128), 1) == (to // 2 % 8) * 16 + (to // 16) * 2 + to % 2).astype(BF)
     by_head = jnp.dot(perm, c1[...].reshape(128, 512), preferred_element_type=F32).astype(BF)
@@ -389,7 +416,7 @@
 
     def rg_sib(last):
         for q in range(4):
-            if (RG2_AT[q] <= 1) != last:
+            if (RG2_AT[q] <= 1 and not SIB_AT) != last:
                 gather_wait(rg, RESIDUAL, rgr, q, 2)
                 send(rg.at[core, q], rg.at[core, q], rbs.at[q], rbr.at[q], sib)
     rg_sib(False)
@@ -466,25 +493,54 @@
     for q in range(4):
         ag[core, q, at["z"], at["y"], at["x"]] = shard[:, q * 128:(q + 1) * 128]
         gather_start(ag, GATHER, ags, agr, q, 0)
-    if not UNPACK_FIRST:
+    def forward(q, j, order):
+        p = (at[order[2]] + j) % 4
+        piece = slab(ag, order, q, 2, p)
+        send(piece, piece, abs_.at[q, p], abr.at[q, p], sib)
+
+    def forwarded(q, order):
+        for p in range(4):
+            landed(slab(ag, order, q, 2, p, 1 - core), abr.at[q, p])
+
+    def forward_left(q, order):
+        for p in range(4):
+            landed(slab(ag, order, q, 2, p), abs_.at[q, p])
+
+    def rg_landed():
         rg_sib(True)
         for q in range(4):
             landed(rg.at[1 - core, q], rbr.at[q])
-    each(UNPACK_FIRST, 16, unpack)
+    if RG_LATE == 0:
+        if not UNPACK_FIRST:
+            rg_landed()
+        each(UNPACK_FIRST, 16, unpack)
     for q in range(4):
         gather_wait(ag, GATHER, agr, q, 0)
         gather_start(ag, GATHER, ags, agr, q, 1)
-    each(0, 8, reorder)
+    if RG_LATE == 1:
+        rg_landed()
+        each(0, 16, unpack)
+    if RG_LATE <= 1:
+        each(0, 8, reorder)
     for q in range(4):
         gather_wait(ag, GATHER, agr, q, 1)
         gather_start(ag, GATHER, ags, agr, q, 2)
+        by_core(GATHER[q], functools.partial(forward, q, 0))
+    if RG_LATE == 2:
+        rg_landed()
+        each(0, 16, unpack)
+        each(0, 8, reorder)
     chosen[...] = jnp.dot(turns[3], marks[...], preferred_element_type=F32)
     landed(wg, ld.at[1])
     landed(wu, ld.at[2])
     activate(1, lax.fori_loop(0, 8, resting, jnp.zeros((128, 1), F32)))
+    def last_slabs(q, order):
+        for j in range(1, 4):
+            p = (at[order[2]] + j) % 4
+            landed(slab(ag, order, q, 2, p), agr.at[q, 2, p])
+            forward(q, j, order)
     for q in range(4):
-        gather_wait(ag, GATHER, agr, q, 2)
-        send(ag.at[core, q], ag.at[core, q], abs_.at[q], abr.at[q], sib)
+        by_core(GATHER[q], functools.partial(last_slabs, q))
 
     def serving(c):
         def step(z, squares):
@@ -502,22 +558,26 @@
         return step
     squares = lax.fori_loop(0, 4, serving(core), jnp.zeros((128, 1), F32))
     for q in range(4):
-        landed(ag.at[1 - core, q], abr.at[q])
+        order = GATHER[q]
+        by_core(order if isinstance(order[0], str) else order[::-1], functools.partial(forwarded, q))
     activate(0, lax.fori_loop(0, 4, serving(1 - core), squares))
 
     lane = iota((256, 128), 1)
     e_own, e_sib = n * 2 + l // 8, sib[0] * 2 + l // 8
     landed(wd.at[0], ld.at[3])
     landed(wd.at[1], wdr)
+
+    ybuf, r1, t1 = (ya, yb, yc), (r1a, r1b, r1c), (t1a, t1b, t1c)
+    r2, t2, r3 = (r2a, r2b, r2c), (t2a, t2b, t2c), (r3a, r3b, r3c)
+    turned = []
+    for k in range(3):
+        m0 = jnp.dot(turns[k], mid[0].reshape(256, 256), preferred_element_type=F32).astype(BF)
+        turned.append((m0, jnp.dot(turns[k], combine[...], preferred_element_type=F32)))
     for half in range(2):
         landed(mid.at[1, half], mr.at[half])
-
-    ybuf, r1, t1 = (ya, yb, yc), (r1a, r1b, r1c), (t1a, t1b, t1c)
-    r2, t2, r3 = (r2a, r2b, r2c), (t2a, t2b, t2c), (r3a, r3b, r3c)
     for k, (lo, width, order) in enumerate(PARTS):
-        m0 = jnp.dot(turns[k], mid[0].reshape(256, 256), preferred_element_type=F32).astype(BF)
+        m0, cw = turned[k]
         m1 = jnp.dot(turns[k], mid[1].reshape(256, 256), preferred_element_type=F32).astype(BF)
-        cw = jnp.dot(turns[k], combine[...], preferred_element_type=F32)
         w0 = jnp.sum(jnp.where(lane == e_own, cw, 0.0), axis=1, keepdims=True)
         w1 = jnp.sum(jnp.where(lane == e_sib, cw, 0.0), axis=1, keepdims=True)
         cn = 384 if width % 384 == 0 else 640
@@ -590,6 +650,9 @@
     each(1, 16, drain)
 
     def drain_home(t):
+        if THROTTLE == 0:
+            cache_left(t)
+
         @pl.when(jnp.logical_not((t == n) & (home_local(t, n) == l)))
         def _():
             landed(q2s.at[t], q2ss.at[t])
@@ -608,7 +671,7 @@
     gather_drain(ag, GATHER, ags)
     for q in range(4):
         landed(rg.at[core, q], rbs.at[q])
-        landed(ag.at[core, q], abs_.at[q])
+        by_core(GATHER[q], functools.partial(forward_left, q))
     landed(wd.at[1], wds)
     for half in range(2):
         landed(mid.at[0, half], ms.at[half])
@@ -654,7 +717,7 @@
         + [dma((k,)) for k in (8, 8, 8, 8, 16, 16)]
         + [
             dma((4, 3, 4)), dma((4, 3, 4)), dma((4,)), dma((4,)),
-            dma((4, 3, 4)), dma((4, 3, 4)), dma((4,)), dma((4,)),
+            dma((4, 3, 4)), dma((4, 3, 4)), dma((4, 4)), dma((4, 4)),
             dma, dma, dma((2,)), dma((2,)), dma((3, 3, 4)), dma((3, 3, 4)), dma, dma,
         ],
         compiler_params=pltpu.CompilerParams(

time: 108 us -> 107 us (level)
  no operation moved by 1% of the time
where the time goes in v4:
time: 107 us
  Pallas kernels  105 us (98%)
  local copies, waits for them, and re-layouts  1.38 us (1%)
    pallas_call x1, Pallas kernels, layer(): pl.pallas_call(kernel, name='layer', out_shape=jax.ShapeDtypeStruct((2, 7...  105 us

profile of v4, /device:TPU:1, one launch (start us, length us, event | category | flops | bytes accessed | tf_op | source)
XLA Modules:
  0.0 106.6 jit_solution(15572110866602970064)
XLA Ops:
  0.0 105.3 %layer.1 = bf16[2,7168]{1,0:T(2,128)(2,1)} custom-call(s32[64]{0:T(128)} %owner.1, s32[64]{0:T(128)} %lengths.1, s32[2,8]{1,0:T(2,128)} %bitcast.17, s32[1,64]{1,0:T(1,128)} %bitcast.16, bf16[2,73728]{1,0:T(2,128)(2,1)} %bitcast.10, bf16[2,576]{1,0:T(2,128)(2,1)} %bitcast.15, bf16[2,7168]{1,0:T(2,128)(2,1)} %bitcast.13, f32[1,7168]{1,0:T(1,128)} %bitcast.14, ...), custom_call_target="tpu_custom_call" | custom-call | tf_op jit(solution)/shard_map/layer/pallas_call | solution.py:693
  105.3 1.4 %copy.16 = bf16[1,2,7168]{2,1,0:T(2,128)(2,1)} copy(bf16[1,2,7168]{2,1,0:T(2,128)(2,1)} %bitcast.12) | data formatting | bytes 57344

commit v5 on v4

--- a/solution.py
+++ b/solution.py
@@ -628,12 +628,13 @@
             landed(r3[k].at[p], rr.at[k, 2, p])
             tot = tot + r3[k][p].astype(F32)
         z16[core, :, lo:lo + width] = tot.astype(BF)
-    send(z16.at[core], z16.at[core], zs, zr, sib)
-    landed(z16.at[1 - core], zr)
+        piece = z16.at[core, :, pl.ds(lo, width)]
+        send(piece, piece, zs.at[k], zr.at[k], sib)
 
     up, dn = iota((16, 16), 0), iota((16, 16), 1)
-    for half in range(2):
-        for k, (lo, width, order) in enumerate(PARTS):
+    for k, (lo, width, order) in enumerate(PARTS):
+        landed(z16.at[1 - core, :, pl.ds(lo, width)], zr.at[k])
+        for half in range(2):
             c0 = half * 3584 + lo
             pickz = ((up < 2) & (dn == at[order[2]] * 4 + core * 2 + up)).astype(BF)
             mix = jnp.dot(pickz, z16[half, :, lo:lo + width], preferred_element_type=F32)
@@ -675,7 +676,8 @@
     landed(wd.at[1], wds)
     for half in range(2):
         landed(mid.at[0, half], ms.at[half])
-    landed(z16.at[core], zs)
+    for k, (lo, width, order) in enumerate(PARTS):
+        landed(z16.at[core, :, pl.ds(lo, width)], zs.at[k])
     for k, (lo, width, order) in enumerate(PARTS):
         for s, buf in enumerate((ybuf[k], t1[k], t2[k])):
             for j in range(1, 4):
@@ -718,7 +720,7 @@
         + [
             dma((4, 3, 4)), dma((4, 3, 4)), dma((4,)), dma((4,)),
             dma((4, 3, 4)), dma((4, 3, 4)), dma((4, 4)), dma((4, 4)),
-            dma, dma, dma((2,)), dma((2,)), dma((3, 3, 4)), dma((3, 3, 4)), dma, dma,
+            dma, dma, dma((2,)), dma((2,)), dma((3, 3, 4)), dma((3, 3, 4)), dma((3,)), dma((3,)),
         ],
         compiler_params=pltpu.CompilerParams(
             collective_id=0, has_side_effects=True, vmem_limit_bytes=58 << 20

time: 107 us -> 107 us (level)
  no operation moved by 1% of the time
where the time goes in v5:
time: 107 us
  Pallas kernels  105 us (98%)
  local copies, waits for them, and re-layouts  1.38 us (1%)
    pallas_call x1, Pallas kernels, layer(): pl.pallas_call(kernel, name='layer', out_shape=jax.ShapeDtypeStruct((2, 7...  105 us

profile of v5, /device:TPU:1, one launch (start us, length us, event | category | flops | bytes accessed | tf_op | source)
XLA Modules:
  0.0 106.6 jit_solution(1062593680021158222)
XLA Ops:
  0.0 105.2 %layer.1 = bf16[2,7168]{1,0:T(2,128)(2,1)} custom-call(s32[64]{0:T(128)} %owner.1, s32[64]{0:T(128)} %lengths.1, s32[2,8]{1,0:T(2,128)} %bitcast.17, s32[1,64]{1,0:T(1,128)} %bitcast.16, bf16[2,73728]{1,0:T(2,128)(2,1)} %bitcast.10, bf16[2,576]{1,0:T(2,128)(2,1)} %bitcast.15, bf16[2,7168]{1,0:T(2,128)(2,1)} %bitcast.13, f32[1,7168]{1,0:T(1,128)} %bitcast.14, ...), custom_call_target="tpu_custom_call" | custom-call | tf_op jit(solution)/shard_map/layer/pallas_call | solution.py:695
  105.2 1.4 %copy.16 = bf16[1,2,7168]{2,1,0:T(2,128)(2,1)} copy(bf16[1,2,7168]{2,1,0:T(2,128)(2,1)} %bitcast.12) | data formatting | bytes 57344
